TPU v7x, 32 devices: a whole 2x2x4 slice. The times are simulated.
32 devices in a mesh: wide: 8 (over z, y), narrow: 4 (over x, core).
Axes of the slice: x: 2, y: 2, z: 4, core: 2. Of those that a mesh axis runs over, the one named last changes fastest.
Arguments:
- tokens: bfloat16 [64, 512, 768], P('wide', 'narrow'), may hold values from -6 to 6
- lengths: int32 [64], P('wide'), may hold values from 16 to 512, as said below
- routes: int32 [64, 512, 1], P('wide', 'narrow'), may hold values from 0 to 7
- bucket_table: int32 [1023], replicated, may hold values from 0 to 31, as said below
- attn_gain: bfloat16 [768], replicated, may hold values from 0.5 to 1.5
- query_weight: bfloat16 [768, 768], replicated, may hold values from -0.0546875 to 0.0546875
- key_weight: bfloat16 [768, 768], replicated, may hold values from -0.21875 to 0.21875
- value_weight: bfloat16 [768, 768], replicated, may hold values from -0.21875 to 0.21875
- output_weight: bfloat16 [768, 768], replicated, may hold values from -1.25 to 1.25
- relative_bias: bfloat16 [32, 12], replicated, may hold values from -3 to 3
- expert_gain: bfloat16 [768], replicated, may hold values from 0.5 to 1.5
- router_weight: bfloat16 [768, 8], replicated, may hold values from -0.15625 to 0.15625
- experts_in: bfloat16 [8, 768, 3072], P('wide'), may hold values from -0.21875 to 0.21875
- experts_out: bfloat16 [8, 3072, 768], P('wide'), may hold values from -0.875 to 0.875
- cotangent: bfloat16 [64, 512, 768], P('wide', 'narrow'), may hold values from -6 to 6
Outputs:
- layer_output: float32 [64, 512, 768], P('wide', 'narrow')
- input_grad: float32 [64, 512, 768], P('wide', 'narrow')
- grad_attn_gain: float32 [768], P('narrow')
- grad_query: float32 [768, 768], P('narrow')
- grad_key: float32 [768, 768], P('narrow')
- grad_value: float32 [768, 768], P('narrow')
- grad_output_weight: float32 [768, 768], P('narrow')
- grad_relative: float32 [32, 12], P('narrow')
- grad_expert_gain: float32 [768], P('narrow')
- grad_router: float32 [768, 8], P('narrow')
- grad_experts_in: float32 [8, 768, 3072], P('wide', 'narrow')
- grad_experts_out: float32 [8, 3072, 768], P('wide', 'narrow')
Inputs may be any that keep to these rules, and one draw needn't show every extreme that they name: lengths[s] counts the valid leading positions of sequence s; some sequence is full in every draw. bucket_table[j - i + 511] is the bucket of key position j seen from query position i.
All inputs are finite; a program needn't handle non-finite values.
Results may differ from a plain program's by a relative error of at most 0.018.
Values may be sent and summed in bfloat16 or wider, within the bound.
A program may use at most 192 MiB of HBM per device.

v0:
```python
import jax
import jax.numpy as jnp
from jax import lax
from jax.sharding import PartitionSpec as P

epsilon = 1e-06
highest_precision = lax.Precision.HIGHEST


def normalize(field, gain_vec):
    inv_rms = lax.rsqrt(jnp.mean(field * field, axis=-1, keepdims=True) + epsilon)
    return (field * inv_rms * gain_vec, inv_rms)


def norm_backward(upstream, field, inv_rms, gain_vec):
    scaled = upstream * gain_vec
    inner_mean = jnp.mean(scaled * field, axis=-1, keepdims=True)
    field_grad = inv_rms * scaled - field * inv_rms**3 * inner_mean
    gain_grad = jnp.sum((upstream * field * inv_rms).reshape(-1, field.shape[-1]), axis=0)
    return (field_grad, gain_grad)


def body(
    tokens,
    lengths,
    routes,
    bucket_table,
    attn_gain,
    query_weight,
    key_weight,
    value_weight,
    output_weight,
    relative_bias,
    expert_gain,
    router_weight,
    experts_in,
    experts_out,
    cotangent,
):
    seq_count, span_len, model_width = tokens.shape
    narrow_n = lax.axis_size("narrow")
    wide_n = lax.axis_size("wide")
    seq_len = span_len * narrow_n
    head_count = relative_bias.shape[1]
    bucket_count = relative_bias.shape[0]
    expert_count = router_weight.shape[1]
    local_experts = experts_in.shape[0]
    hidden_units = experts_in.shape[2]
    tok_count = seq_count * span_len
    capacity = 5 * tok_count // (4 * expert_count)
    token_f = tokens.astype(jnp.float32)
    gain_attn = attn_gain.astype(jnp.float32)
    gain_expert = expert_gain.astype(jnp.float32)
    normed_f, inv_first = normalize(token_f, gain_attn)
    normed = normed_f.astype(jnp.bfloat16)
    queries = jnp.dot(normed, query_weight, preferred_element_type=jnp.float32).astype(jnp.bfloat16)
    keys_local = jnp.dot(normed, key_weight, preferred_element_type=jnp.float32).astype(
        jnp.bfloat16
    )
    values_local = jnp.dot(normed, value_weight, preferred_element_type=jnp.float32).astype(
        jnp.bfloat16
    )
    keys_all, values_all = (
        lax.all_gather(keys_local, "narrow", axis=1, tiled=True),
        lax.all_gather(values_local, "narrow", axis=1, tiled=True),
    )
    first_row = lax.axis_index("narrow") * span_len
    query_rows = first_row + jnp.arange(span_len, dtype=jnp.int32)
    key_cols = jnp.arange(seq_len, dtype=jnp.int32)
    bucket_rows = bucket_table[key_cols[None, :] - query_rows[:, None] + seq_len - 1]
    score_bias = relative_bias.astype(jnp.float32)[bucket_rows].transpose(2, 0, 1)
    key_valid = key_cols[None, :] < lengths[:, None]

    def scores_of(seq_query, seq_keys, seq_valid):
        split_q = seq_query.reshape(span_len, head_count, -1)
        split_k = seq_keys.reshape(seq_len, head_count, -1)
        scores = (
            jnp.einsum("chd,jhd->hcj", split_q, split_k, preferred_element_type=jnp.float32)
            + score_bias
        )
        return jnp.where(seq_valid[None, None, :], scores, -1e30)

    def forward_one(item):
        seq_query, seq_keys, seq_values, seq_valid = item
        scores = scores_of(seq_query, seq_keys, seq_valid)
        row_max = jnp.max(scores, axis=-1, keepdims=True)
        log_total = row_max + jnp.log(jnp.sum(jnp.exp(scores - row_max), axis=-1, keepdims=True))
        prob_low = jnp.exp(scores - log_total).astype(jnp.bfloat16)
        split_v = seq_values.reshape(seq_len, head_count, -1)
        mixed = jnp.einsum("hcj,jhd->chd", prob_low, split_v, preferred_element_type=jnp.float32)
        return (mixed.reshape(span_len, model_width).astype(jnp.bfloat16), log_total[..., 0])

    attended, log_totals = lax.map(forward_one, (queries, keys_all, values_all, key_valid))
    branch = jnp.dot(attended, output_weight, preferred_element_type=jnp.float32)
    hidden = token_f + branch
    routed_f, inv_second = normalize(hidden, gain_expert)
    routed = routed_f.astype(jnp.bfloat16).reshape(tok_count, model_width)
    logits = jnp.dot(routed, router_weight, preferred_element_type=jnp.float32)
    prob_rows = jax.nn.softmax(logits, axis=-1)
    route_ids = routes.reshape(tok_count)
    onehot = route_ids[:, None] == jnp.arange(expert_count, dtype=jnp.int32)[None, :]
    gate = jnp.sum(jnp.where(onehot, prob_rows, 0.0), axis=-1)
    counts = jnp.cumsum(onehot.astype(jnp.int32), axis=0)
    position = jnp.sum(jnp.where(onehot, counts - 1, 0), axis=-1)
    kept_mask = position < capacity
    slot_index = jnp.where(kept_mask, route_ids * capacity + position, expert_count * capacity)
    safe_index = jnp.minimum(slot_index, expert_count * capacity - 1)
    send_rows = jnp.zeros((expert_count * capacity, model_width), jnp.bfloat16)
    send_rows = (
        send_rows.at[slot_index]
        .set(routed, mode="drop")
        .reshape(expert_count, capacity, model_width)
    )
    received = lax.all_to_all(send_rows, "wide", split_axis=0, concat_axis=0, tiled=True)
    item_count = received.shape[1]
    grouped = received.reshape(wide_n, local_experts, item_count, model_width)
    pre_act = jnp.einsum("sxcd,xdf->sxcf", grouped, experts_in, preferred_element_type=jnp.float32)
    activation = jax.nn.gelu(pre_act).astype(jnp.bfloat16)
    result = jnp.einsum(
        "sxcf,xfd->sxcd", activation, experts_out, preferred_element_type=jnp.float32
    )
    result = result.astype(jnp.bfloat16).reshape(expert_count, item_count, model_width)
    returned_rows = lax.all_to_all(result, "wide", split_axis=0, concat_axis=0, tiled=True)
    activ_kept = activation.reshape(expert_count, item_count, hidden_units)
    pre_kept = pre_act.reshape(expert_count, item_count, hidden_units)
    expert_tok = jnp.where(
        kept_mask[:, None],
        returned_rows.reshape(expert_count * capacity, model_width)[safe_index].astype(jnp.float32),
        0.0,
    )
    out_grad = cotangent.astype(jnp.float32)
    flat_grad = out_grad.reshape(tok_count, model_width)
    layer_output = hidden + (gate[:, None] * expert_tok).reshape(seq_count, span_len, model_width)
    gate_grad = jnp.sum(flat_grad * expert_tok, axis=-1)
    slot_grad = (gate[:, None] * flat_grad).astype(jnp.bfloat16)
    grad_rows = jnp.zeros((expert_count * capacity, model_width), jnp.bfloat16)
    grad_rows = (
        grad_rows.at[slot_index]
        .set(slot_grad, mode="drop")
        .reshape(expert_count, capacity, model_width)
    )
    result_grad = lax.all_to_all(grad_rows, "wide", split_axis=0, concat_axis=0, tiled=True)
    result_four = result_grad.reshape(wide_n, local_experts, capacity, model_width)
    activ_four = activ_kept.reshape(wide_n, local_experts, capacity, hidden_units)
    pre_four = pre_kept.reshape(wide_n, local_experts, capacity, hidden_units)
    arrived_four = received.reshape(wide_n, local_experts, capacity, model_width)
    activ_grad = jnp.einsum(
        "sxcd,xfd->sxcf", result_four, experts_out, preferred_element_type=jnp.float32
    )
    gelu_pull = jax.vjp(jax.nn.gelu, pre_four)[1]
    pre_grad = gelu_pull(activ_grad)[0].astype(jnp.bfloat16)
    input_rows = jnp.einsum(
        "sxcf,xdf->sxcd", pre_grad, experts_in, preferred_element_type=jnp.float32
    )
    input_rows = input_rows.astype(jnp.bfloat16).reshape(expert_count, capacity, model_width)
    back_rows = lax.all_to_all(input_rows, "wide", split_axis=0, concat_axis=0, tiled=True)
    term_in = jnp.einsum(
        "sxcd,sxcf->xdf", arrived_four, pre_grad, preferred_element_type=jnp.float32
    )
    term_out = jnp.einsum(
        "sxcf,sxcd->xfd", activ_four, result_four, preferred_element_type=jnp.float32
    )
    grad_experts_in, grad_experts_out = (
        lax.psum_scatter(
            term_in.astype(jnp.bfloat16), "narrow", scatter_dimension=1, tiled=True
        ).astype(jnp.float32),
        lax.psum_scatter(
            term_out.astype(jnp.bfloat16), "narrow", scatter_dimension=1, tiled=True
        ).astype(jnp.float32),
    )
    prob_push = jnp.where(onehot, gate_grad[:, None], 0.0)
    logit_grad = (prob_rows * (prob_push - (gate * gate_grad)[:, None])).astype(jnp.bfloat16)
    router_grad = jnp.einsum("td,te->de", routed, logit_grad, preferred_element_type=jnp.float32)
    routed_grad = jnp.einsum(
        "te,de->td", logit_grad, router_weight, preferred_element_type=jnp.float32
    )
    routed_grad = routed_grad + jnp.where(
        kept_mask[:, None],
        back_rows.reshape(expert_count * capacity, model_width)[safe_index].astype(jnp.float32),
        0.0,
    )
    hidden_part, gain_second = norm_backward(
        routed_grad.reshape(seq_count, span_len, model_width), hidden, inv_second, gain_expert
    )
    hidden_grad = out_grad + hidden_part
    branch_grad = hidden_grad.astype(jnp.bfloat16)
    output_grad = jnp.einsum(
        "scd,sce->de", attended, branch_grad, preferred_element_type=jnp.float32
    )
    attended_grad = jnp.einsum(
        "sce,de->scd", branch_grad, output_weight, preferred_element_type=jnp.float32
    ).astype(jnp.bfloat16)
    keys_back, values_back = (keys_all, values_all)

    def backward_one(bias_total, item):
        seq_query, seq_keys, seq_values, seq_valid, seq_total, seq_grad = item
        scores = scores_of(seq_query, seq_keys, seq_valid)
        prob_seq = jnp.exp(scores - seq_total[..., None])
        split_q = seq_query.reshape(span_len, head_count, -1)
        split_k = seq_keys.reshape(seq_len, head_count, -1)
        split_v = seq_values.reshape(seq_len, head_count, -1)
        split_g = seq_grad.reshape(span_len, head_count, -1)
        prob_grad = jnp.einsum("chd,jhd->hcj", split_g, split_v, preferred_element_type=jnp.float32)
        delta_sum = jnp.sum(prob_seq * prob_grad, axis=-1, keepdims=True)
        score_grad = (prob_seq * (prob_grad - delta_sum)).astype(jnp.bfloat16)
        query_part = jnp.einsum(
            "hcj,jhd->chd", score_grad, split_k, preferred_element_type=jnp.float32
        )
        new_total = bias_total + score_grad.astype(jnp.float32)
        key_part = jnp.einsum(
            "hcj,chd->jhd", score_grad, split_q, preferred_element_type=jnp.float32
        )
        value_part = jnp.einsum(
            "hcj,chd->jhd",
            prob_seq.astype(jnp.bfloat16),
            split_g,
            preferred_element_type=jnp.float32,
        )
        return (
            new_total,
            (
                query_part.reshape(span_len, model_width),
                key_part.reshape(seq_len, model_width),
                value_part.reshape(seq_len, model_width),
            ),
        )

    bias_start = jnp.zeros((head_count, span_len, seq_len), jnp.float32)
    bias_total, scanned = lax.scan(
        backward_one,
        bias_start,
        (queries, keys_back, values_back, key_valid, log_totals, attended_grad),
    )
    query_grad, key_terms, value_terms = scanned
    key_sum, value_sum = (
        lax.psum_scatter(
            key_terms.astype(jnp.bfloat16), "narrow", scatter_dimension=1, tiled=True
        ).astype(jnp.float32),
        lax.psum_scatter(
            value_terms.astype(jnp.bfloat16), "narrow", scatter_dimension=1, tiled=True
        ).astype(jnp.float32),
    )
    query_low = query_grad.astype(jnp.bfloat16)
    key_low = key_sum.astype(jnp.bfloat16)
    value_low = value_sum.astype(jnp.bfloat16)
    grad_query = jnp.einsum("scd,sce->de", normed, query_low, preferred_element_type=jnp.float32)
    grad_key = jnp.einsum("scd,sce->de", normed, key_low, preferred_element_type=jnp.float32)
    grad_value = jnp.einsum("scd,sce->de", normed, value_low, preferred_element_type=jnp.float32)
    normed_grad = jnp.einsum(
        "sce,de->scd", query_low, query_weight, preferred_element_type=jnp.float32
    )
    normed_grad = normed_grad + jnp.einsum(
        "sce,de->scd", key_low, key_weight, preferred_element_type=jnp.float32
    )
    normed_grad = normed_grad + jnp.einsum(
        "sce,de->scd", value_low, value_weight, preferred_element_type=jnp.float32
    )
    input_part, gain_first = norm_backward(normed_grad, token_f, inv_first, gain_attn)
    input_grad = hidden_grad + input_part
    bucket_onehot = (
        bucket_rows.reshape(-1)[:, None] == jnp.arange(bucket_count, dtype=jnp.int32)[None, :]
    ).astype(jnp.float32)
    relative_grad = jnp.einsum(
        "hn,nb->bh", bias_total.reshape(head_count, -1), bucket_onehot, precision=highest_precision
    )
    shares = (
        lax.psum_scatter(
            grad_query.astype(jnp.bfloat16), "narrow", scatter_dimension=0, tiled=True
        ).astype(jnp.float32),
        lax.psum_scatter(
            grad_key.astype(jnp.bfloat16), "narrow", scatter_dimension=0, tiled=True
        ).astype(jnp.float32),
        lax.psum_scatter(
            grad_value.astype(jnp.bfloat16), "narrow", scatter_dimension=0, tiled=True
        ).astype(jnp.float32),
        lax.psum_scatter(
            output_grad.astype(jnp.bfloat16), "narrow", scatter_dimension=0, tiled=True
        ).astype(jnp.float32),
        lax.psum_scatter(
            router_grad.astype(jnp.bfloat16), "narrow", scatter_dimension=0, tiled=True
        ).astype(jnp.float32),
        lax.psum_scatter(
            relative_grad.astype(jnp.bfloat16), "narrow", scatter_dimension=0, tiled=True
        ).astype(jnp.float32),
        lax.psum_scatter(
            gain_first.astype(jnp.bfloat16), "narrow", scatter_dimension=0, tiled=True
        ).astype(jnp.float32),
        lax.psum_scatter(
            gain_second.astype(jnp.bfloat16), "narrow", scatter_dimension=0, tiled=True
        ).astype(jnp.float32),
    )
    totals = lax.psum(
        (shares[0], shares[1], shares[2], shares[3], shares[4], shares[5], shares[6], shares[7]),
        "wide",
    )
    return (
        layer_output,
        input_grad,
        totals[6],
        totals[0],
        totals[1],
        totals[2],
        totals[3],
        totals[5],
        totals[7],
        totals[4],
        grad_experts_in,
        grad_experts_out,
    )


def solution(mesh):
    return jax.shard_map(
        body,
        mesh=mesh,
        in_specs=(
            P("wide", "narrow", None),
            P("wide"),
            P("wide", "narrow", None),
            P(),
            P(),
            P(),
            P(),
            P(),
            P(),
            P(),
            P(),
            P(),
            P("wide", None, None),
            P("wide", None, None),
            P("wide", "narrow", None),
        ),
        out_specs=(
            P("wide", "narrow", None),
            P("wide", "narrow", None),
            P("narrow"),
            P("narrow", None),
            P("narrow", None),
            P("narrow", None),
            P("narrow", None),
            P("narrow", None),
            P("narrow"),
            P("narrow", None),
            P("wide", "narrow", None),
            P("wide", "narrow", None),
        ),
        check_vma=False,
    )
```

profile of v0, /device:TPU:0, one launch (start us, length us, event | category | flops | bytes accessed | tf_op | source)
XLA Modules:
  0.0 1409.9 jit_solution(17103949652462044249)
XLA Ops:
  21.9 260.7 %gather_fusion = s32[65536]{0:T(1024)S(1)} fusion(s32[1023]{0:T(1024)S(1)} %copy-done.1, s32[65536]{0:T(1024)S(1)} %broadcast_clamp_fusion.1), kind=kCustom, calls=%fused_computation | custom fusion | bytes 786432 | tf_op jit(solution)/shard_map/gather | solution.py:70
  289.3 215.5 %gather_fusion.1 = f32[65536,12]{1,0:T(8,128)} fusion(f32[32,12]{1,0:T(8,128)S(1)} %copy.107, s32[65536]{0:T(1024)S(1)} %broadcast_clamp_fusion), kind=kCustom, calls=%fused_computation.1 | custom fusion | bytes 6553600 | tf_op jit(solution)/shard_map/gather | solution.py:71
  504.8 20.7 %copy.108 = f32[128,512,12]{1,0,2:T(8,128)} copy(f32[128,512,12]{2,1,0:T(8,128)} %bitcast.309) | data formatting | bytes 6291456 | tf_op jit(solution)/shard_map/gather | solution.py:71
  543.2 51.0 %while.29 = (s32[]{:T(128)}, bf16[8,128,768]{1,2,0:T(8,128)(2,1)}, f32[8,12,128]{2,1,0:T(8,128)}, bf16[8,512,768]{1,2,0:T(8,128)(2,1)}, pred[8,512]{1,0:T(8,128)...) while((s32[]{:T(128)}, bf16[8,128,768]{1,2,0:T(8,128)(2,1)}, ...), condition=%wide.region_4.5_spmd, body=%wide.region_1.4_spmd.sunk | while | flops 206928384 | bytes 31116948 | solution.py:93
  622.6 36.5 %all-to-all-done = bf16[8,160,768]{2,1,0:T(8,128)(2,1)} async-done(((bf16[8,160,768]{2,1,0:T(8,128)(2,1)}), bf16[8,160,768]{2,1,0:T(8,128)(2,1)}, u32[]{:S(2)}, u32[]{:S(2)}) %all-to-all-start) | async-done | bytes 1966112 | tf_op jit(solution)/shard_map/all_to_all | solution.py:114
  677.0 12.6 fusion.60
  689.6 18.8 %all-to-all-done.2 = bf16[8,160,768]{2,1,0:T(8,128)(2,1)S(1)} async-done(((bf16[8,160,768]{2,1,0:T(8,128)(2,1)}), bf16[8,160,768]{2,1,0:T(8,128)(2,1)S(1)}, u32[]{:S(2)}, u32[]{:S(2)}) %all-to-all-start.2) | async-done | bytes 1966112 | tf_op jit(solution)/shard_map/all_to_all | solution.py:142
  713.7 19.1 %fusion.11 = bf16[8,1,160,3072]{3,2,0,1:T(8,128)(2,1)S(1)} fusion(f32[8,160,3072]{2,1,0:T(8,128)} %copy-done.43, bf16[8,160,768]{2,1,0:T(8,128)(2,1)} %copy-done.20, bf16[1,3072,768]{2,1,0:T(8,128)(2,1)} %param.32), kind=kOutput, calls=%fused_computation.42 | convolution fusion | flops 6118440960 | bytes 30277632 | tf_op jit(solution)/shard_map/sxcd,xfd->sxcf/dot_general | solution.py:147
  735.9 9.8 fusion.65
  745.7 13.6 all-to-all-done.1
  771.9 36.8 %all-to-all-done.3 = bf16[8,160,768]{2,1,0:T(8,128)(2,1)} async-done(((bf16[8,160,768]{2,1,0:T(8,128)(2,1)}), bf16[8,160,768]{2,1,0:T(8,128)(2,1)}, u32[]{:S(2)}, u32[]{:S(2)}) %all-to-all-start.3) | async-done | bytes 1966112 | tf_op jit(solution)/shard_map/all_to_all | solution.py:156
  823.8 105.1 %while.30 = (s32[]{:T(128)}, f32[12,128,512]{2,1,0:T(8,128)}, bf16[8,128,768]{1,2,0:T(8,128)(2,1)}, bf16[8,512,768]{1,2,0:T(8,128)(2,1)}, bf16[8,512,768]{1,2,0:...) while((s32[]{:T(128)}, f32[12,128,512]{2,1,0:T(8,128)}, ...), condition=%wide.region_18.19_spmd.clone, body=%wide.region_16.18_spmd.clone.sunk | while | flops 512752128 | bytes 83590920 | solution.py:229
  928.9 9.2 copy.139
  946.1 9.8 copy.137
  975.7 13.8 fusion.40
  989.6 10.8 fusion.37
  1015.1 49.1 %reduce-scatter.28.cloned.1.call-done = bf16[128,6144]{1,0:T(8,128)(2,1)} async-done(((bf16[512,6144]{1,0:T(8,128)(2,1)}), bf16[128,6144]{1,0:T(8,128)(2,1)}) %reduce-scatter.28.cloned.1.call-update) | async-done | bytes 1572880
  1087.6 27.3 %reduce-scatter.22.cloned.1.call-done = bf16[192,768]{1,0:T(8,128)(2,1)} async-done(((bf16[768,768]{1,0:T(8,128)(2,1)}), bf16[192,768]{1,0:T(8,128)(2,1)}) %reduce-scatter.22.cloned.1.call-update) | async-done | bytes 294928 | tf_op jit(solution)/shard_map/reduce_scatter | solution.py:276
  1114.9 29.1 %reduce-scatter.16.cloned.1.call-done = bf16[192,768]{1,0:T(8,128)(2,1)} async-done(((bf16[768,768]{1,0:T(8,128)(2,1)}), bf16[192,768]{1,0:T(8,128)(2,1)}) %reduce-scatter.16.cloned.1.call-update) | async-done | bytes 294928 | tf_op jit(solution)/shard_map/reduce_scatter | solution.py:267
  1144.0 50.4 %reduce-scatter.26.cloned.1.call-done = bf16[1,768,768]{2,1,0:T(8,128)(2,1)} async-done(((bf16[1,3072,768]{2,1,0:T(8,128)(2,1)}), bf16[1,768,768]{2,1,0:T(8,128)(2,1)}) %reduce-scatter.26.cloned.1.call-update) | async-done | bytes 1179664 | tf_op jit(solution)/shard_map/reduce_scatter | solution.py:167
  1197.3 47.7 %reduce-scatter.24.cloned.1.call-done = bf16[1,192,3072]{2,1,0:T(8,128)(2,1)} async-done(((bf16[1,768,3072]{2,1,0:T(8,128)(2,1)}), bf16[1,192,3072]{2,1,0:T(8,128)(2,1)}) %reduce-scatter.24.cloned.1.call-update) | async-done | bytes 1179664 | tf_op jit(solution)/shard_map/reduce_scatter | solution.py:164
  1254.4 10.1 all-reduce.4
  1273.2 28.5 %reduce-scatter.18.cloned.1.call-done = bf16[192,768]{1,0:T(8,128)(2,1)} async-done(((bf16[768,768]{1,0:T(8,128)(2,1)}), bf16[192,768]{1,0:T(8,128)(2,1)}) %reduce-scatter.18.cloned.1.call-update) | async-done | bytes 294928 | tf_op jit(solution)/shard_map/reduce_scatter | solution.py:270
  1301.6 101.5 %all-reduce.6 = (f32[192]{0:T(256)}, f32[192,768]{1,0:T(8,128)}, f32[192,768]{1,0:T(8,128)}, f32[192,768]{1,0:T(8,128)}, f32[192,768]{1,0:T(8,128)}, /*index=5*/...) all-reduce(f32[192]{0:T(256)S(1)} %get-tuple-element.346, ...), channel_id=1, replica_groups=mesh['wide'=8,'narrow'=4] {'wide'}, use_global_device_ids=true, to_apply=%region_24.25 | all-reduce | flops 591840 | bytes 3552000 | tf_op jit(solution)/shard_map/psum | solution.py:292
  (443 shorter events, 361.7 us)
Async XLA Ops:
  7.2 518.6 %all-gather.5.cloned.1.call-start = ((), (), s32[]{:S(2)}) async-start(), calls=%async_computation.14 | async-start | bytes 7864320 | tf_op jit(solution)/shard_map/all_gather | solution.py:64
  8.0 274.8 %copy-start.33 = (f32[768]{0:T(1024)}, f32[768]{0:T(1024)S(1)}, u32[]{:S(2)}) copy-start(f32[768]{0:T(1024)S(1)} %convert_element_type.185) | copy-start | bytes 9220
  10.4 272.4 %copy-start.31 = (f32[8,128]{1,0:T(8,128)}, f32[8,128]{1,0:T(8,128)S(1)}, u32[]{:S(2)}) copy-start(f32[8,128]{1,0:T(8,128)S(1)} %get-tuple-element.337) | copy-start | bytes 12292
  14.9 519.6 %all-gather.3.cloned.1.call-start = ((), (), s32[]{:S(2)}) async-start(), calls=%async_computation.13 | async-start | bytes 7864320 | tf_op jit(solution)/shard_map/all_gather | solution.py:65
  504.8 20.8 %copy-start.24 = (s32[8,8,128]{2,1,0:T(8,128)S(1)}, s32[8,8,128]{2,1,0:T(8,128)}, u32[]{:S(2)}) copy-start(s32[8,8,128]{2,1,0:T(8,128)} %copy-done.23) | copy-start | bytes 98308
  504.8 20.8 %copy-start.36 = (s32[8,9]{1,0:T(8,128)S(1)}, s32[8,9]{1,0:T(8,128)}, u32[]{:S(2)}) copy-start(s32[8,9]{1,0:T(8,128)} %reduce-window.9) | copy-start | bytes 868
  504.8 20.8 %copy-start.28 = (s32[8,128,1]{1,2,0:T(1,128)S(1)}, s32[8,128,1]{1,2,0:T(1,128)}, u32[]{:S(2)}) copy-start(s32[8,128,1]{1,2,0:T(1,128)} %param.21) | copy-start | bytes 12292
  504.8 20.9 %copy-start.40 = (s32[8]{0:T(128)S(1)}, s32[8]{0:T(128)}, u32[]{:S(2)}) copy-start(s32[8]{0:T(128)} %param.20) | copy-start | bytes 100
  599.6 14.5 %copy-start.11 = (bf16[8,128,768]{2,1,0:T(8,128)(2,1)}, bf16[8,128,768]{2,1,0:T(8,128)(2,1)S(1)}, u32[]{:S(2)}) copy-start(bf16[8,128,768]{2,1,0:T(8,128)(2,1)S(1)} %multiply_convert_fusion.1) | copy-start | bytes 4718596
  606.3 52.8 %all-to-all-start = ((bf16[8,160,768]{2,1,0:T(8,128)(2,1)}), bf16[8,160,768]{2,1,0:T(8,128)(2,1)}, u32[]{:S(2)}, u32[]{:S(2)}) async-start(bf16[8,160,768]{2,1,0:T(8,128)(2,1)} %bitcast.334), calls=%async_computation | async-start | bytes 3932160 | tf_op jit(solution)/shard_map/all_to_all | solution.py:114
  659.1 49.2 %all-to-all-start.2 = ((bf16[8,160,768]{2,1,0:T(8,128)(2,1)}), bf16[8,160,768]{2,1,0:T(8,128)(2,1)S(1)}, u32[]{:S(2)}, u32[]{:S(2)}) async-start(bf16[8,160,768]{2,1,0:T(8,128)(2,1)} %bitcast.37), calls=%async_computation.2 | async-start | bytes 3932160 | tf_op jit(solution)/shard_map/all_to_all | solution.py:142
  709.6 49.6 %all-to-all-start.1 = ((bf16[8,160,768]{2,1,0:T(8,128)(2,1)}), bf16[8,160,768]{2,1,0:T(8,128)(2,1)S(1)}, u32[]{:S(2)}, u32[]{:S(2)}) async-start(bf16[8,160,768]{2,1,0:T(8,128)(2,1)} %fusion.60), calls=%async_computation.1 | async-start | bytes 3932160 | tf_op jit(solution)/shard_map/all_to_all | solution.py:123
  759.3 49.4 %all-to-all-start.3 = ((bf16[8,160,768]{2,1,0:T(8,128)(2,1)}), bf16[8,160,768]{2,1,0:T(8,128)(2,1)}, u32[]{:S(2)}, u32[]{:S(2)}) async-start(bf16[8,160,768]{2,1,0:T(8,128)(2,1)} %fusion.65), calls=%async_computation.3 | async-start | bytes 3932160 | tf_op jit(solution)/shard_map/all_to_all | solution.py:156
  763.6 239.6 %reduce-scatter.30.cloned.1.call-start = ((), (), s32[]{:S(2)}) async-start(), calls=%async_computation.22 | async-start | bytes 7864320
  945.6 118.5 %reduce-scatter.28.cloned.1.call-start = ((), (), s32[]{:S(2)}) async-start(), calls=%async_computation.21 | async-start | bytes 7864320
  963.7 123.1 %reduce-scatter.32.cloned.1.call-start = ((), (), s32[]{:S(2)}) async-start(), calls=%async_computation.23 | async-start | bytes 245760
  966.3 148.7 %reduce-scatter.22.cloned.1.call-start = ((), (), s32[]{:S(2)}) async-start(), calls=%async_computation.18 | async-start | bytes 1474560 | tf_op jit(solution)/shard_map/reduce_scatter | solution.py:276
  971.4 172.6 %reduce-scatter.16.cloned.1.call-start = ((), (), s32[]{:S(2)}) async-start(), calls=%async_computation.15 | async-start | bytes 1474560 | tf_op jit(solution)/shard_map/reduce_scatter | solution.py:267
  975.6 218.8 %reduce-scatter.26.cloned.1.call-start = ((), (), s32[]{:S(2)}) async-start(), calls=%async_computation.20 | async-start | bytes 5898240 | tf_op jit(solution)/shard_map/reduce_scatter | solution.py:167
  989.5 255.5 %reduce-scatter.24.cloned.1.call-start = ((), (), s32[]{:S(2)}) async-start(), calls=%async_computation.19 | async-start | bytes 5898240 | tf_op jit(solution)/shard_map/reduce_scatter | solution.py:164
  1000.4 272.8 %reduce-scatter.20.cloned.1.call-start = ((), (), s32[]{:S(2)}) async-start(), calls=%async_computation.17 | async-start | bytes 1474560 | tf_op jit(solution)/shard_map/reduce_scatter | solution.py:273
  1013.1 288.5 %reduce-scatter.18.cloned.1.call-start = ((), (), s32[]{:S(2)}) async-start(), calls=%async_computation.16 | async-start | bytes 1474560 | tf_op jit(solution)/shard_map/reduce_scatter | solution.py:270
  1264.6 37.0 %copy-start.25 = (bf16[192,768]{1,0:T(8,128)(2,1)S(1)}, bf16[192,768]{1,0:T(8,128)(2,1)}, u32[]{:S(2)}) copy-start(bf16[192,768]{1,0:T(8,128)(2,1)} %reduce-scatter.22.cloned.1.call-done) | copy-start | bytes 884740
  1264.6 37.0 %copy-start.26 = (bf16[192,768]{1,0:T(8,128)(2,1)S(1)}, bf16[192,768]{1,0:T(8,128)(2,1)}, u32[]{:S(2)}) copy-start(bf16[192,768]{1,0:T(8,128)(2,1)} %reduce-scatter.16.cloned.1.call-done) | copy-start | bytes 884740
  (64 other events, 206.7 us)
Sparse Core Ops, SparseCore 0:
  15.0 49.0 all-gather.4
  66.3 46.3 all-gather.2
  945.7 57.3 reduce-scatter.29
  1005.7 58.3 reduce-scatter.27
  1067.0 19.7 reduce-scatter.31
  1089.2 25.6 reduce-scatter.21
  1118.2 25.7 reduce-scatter.15
  1146.5 47.8 reduce-scatter.25
  1197.1 47.8 reduce-scatter.23
  1247.4 25.7 reduce-scatter.19
  1275.9 25.7 reduce-scatter.17
where the time goes:
time: 1420 us; the launch traced here: 1410 us
  local copies, waits for them, and re-layouts  707 us (50%)
  waiting for transfers between devices  345 us (24%)
  matrix products  163 us (11%)
  blocking collectives  112 us (8%)
  other arithmetic  46.5 us (3%)
  starting transfers between devices  20.4 us (1%)
  between operations  16.1 us (1%)
    gather x2, local copies, waits for them, and re-layouts, body(): bucket_table[key_cols[None, :] - query_rows[:, None] + seq_len - 1]  261 us
    gather x2, local copies, waits for them, and re-layouts, body(): relative_bias.astype(jnp.float32)[bucket_rows].transpose(2, 0, 1)  236 us
    psum x1, blocking collectives, body(): lax.psum((shares[0], shares[1], shares[2], shares[3], shares[4], shares[5...  101 us
    unnamed x97, local copies, waits for them, and re-layouts  66.5 us
    dynamic_slice x72, local copies, waits for them, and re-layouts, body(): lax.map(forward_one, (queries, keys_all, values_all, key_valid))  57.6 us
    unnamed x14, waiting for transfers between devices  52.3 us
    reduce_scatter x1, waiting for transfers between devices, body(): lax.psum_scatter(term_out.astype(jnp.bfloat16), 'narrow', scatter_dimensi...  50.4 us
    reduce_scatter x1, waiting for transfers between devices, body(): lax.psum_scatter(term_in.astype(jnp.bfloat16), 'narrow', scatter_dimensio...  47.7 us
  transfers between devices with their start and end apart: 15, of which 13 were waited for; matrix products, arithmetic and copies ran while one was open for 49% of the time, Pallas kernels for 0%

commit v1 on v0

v1 whole, which is shorter than its diff:
```python
import functools

import jax
import jax.numpy as jnp
from jax import lax
from jax.experimental import pallas as pl
from jax.experimental.pallas import tpu as pltpu
from jax.sharding import PartitionSpec as P

f32, bf16 = jnp.float32, jnp.bfloat16
epsilon = 1e-06
VMEM_BYTES = 60 * 1024 * 1024
NN = (((1,), (0,)), ((), ()))
NT = (((1,), (1,)), ((), ()))
TN = (((0,), (0,)), ((), ()))


def dot(a, b, dims=NN):
    return lax.dot_general(a, b, dims, preferred_element_type=f32)


def vmem():
    return pl.BlockSpec(memory_space=pltpu.VMEM)


def params(**kw):
    return pltpu.CompilerParams(vmem_limit_bytes=VMEM_BYTES, **kw)


def inverse_rms(field):
    return lax.rsqrt(jnp.mean(field * field, axis=-1, keepdims=True) + epsilon)


def half_masks(pair_width):
    lane = lax.broadcasted_iota(jnp.int32, (1, pair_width), 1)
    low = lane < pair_width // 2
    return low, (low.astype(f32).astype(bf16), (~low).astype(f32).astype(bf16))


def attention_forward_kernel(
    lens_ref, tok_ref, diag_ref, gain_ref, wq_ref, wk_ref, wv_ref,
    att_ref, q_ref, k_ref, v_ref, p_ref, strip_ref,
):
    pair = pl.program_id(0)
    parts, seqs, span, width = tok_ref.shape
    total = parts * span
    table = diag_ref.shape[-1]
    me = lax.axis_index("narrow")

    @pl.when(pair == 0)
    def _():
        gain = gain_ref[...]

        def project(step, carry):
            s, n = step // (parts // 2), step % (parts // 2)
            x = tok_ref[pl.ds(2 * n, 2), s].reshape(2 * span, width).astype(f32)
            normed = (x * inverse_rms(x) * gain).astype(bf16)
            rows = pl.ds(pl.multiple_of(n * 2 * span, 2 * span), 2 * span)
            q_ref[s, rows, :] = dot(normed, wq_ref[...]).astype(bf16)
            k_ref[s, rows, :] = dot(normed, wk_ref[...]).astype(bf16)
            v_ref[s, rows, :] = dot(normed, wv_ref[...]).astype(bf16)
            return carry

        lax.fori_loop(0, seqs * (parts // 2), project, 0)

    low, masks = half_masks(128)
    for hh in range(2):
        row = diag_ref[0, hh : hh + 1, :]
        strip_ref[hh] = pltpu.roll(
            jnp.broadcast_to(row, (span, table)), table - span + 1, 1, stride=1, stride_axis=0
        )
    lanes = pl.ds(pl.multiple_of(pair * 128, 128), 128)
    cols = lax.broadcasted_iota(jnp.int32, (1, total), 1)

    def one_sequence(s, carry):
        kp = k_ref[s, :, lanes]
        vp = v_ref[s, :, lanes]
        length = lens_ref[me * seqs + s]
        push = jnp.where(cols < length, 0.0, -1e30)
        for block in range(parts // 2):
            rows = slice(block * 2 * span, (block + 1) * 2 * span)
            qp = q_ref[s, rows, lanes]
            mixed = None
            for hh in range(2):
                bias = jnp.concatenate(
                    [
                        strip_ref[hh, :, (parts - 1 - r) * span : (parts - 1 - r) * span + total]
                        for r in (2 * block, 2 * block + 1)
                    ],
                    axis=0,
                )
                scores = dot(qp * masks[hh], kp, NT) + bias + push
                raised = jnp.exp(scores - jnp.max(scores, axis=-1, keepdims=True))
                prob = raised * (1.0 / jnp.sum(raised, axis=-1, keepdims=True))
                prob = prob.astype(bf16)
                p_ref[s, hh, rows, :] = prob
                part = dot(prob, vp)
                mixed = part if hh == 0 else jnp.where(low, mixed, part)
            mixed = mixed.astype(bf16)
            for r in range(2):
                att_ref[2 * block + r, s, :, lanes] = mixed[r * span : (r + 1) * span]
        return carry

    lax.fori_loop(0, seqs, one_sequence, 0)


def attention_forward(lens, tok, diag, gain, wq, wk, wv):
    parts, seqs, span, width = tok.shape
    pairs, _, table = diag.shape
    total = parts * span
    rows = jax.ShapeDtypeStruct((seqs, total, width), bf16)
    return pl.pallas_call(
        attention_forward_kernel,
        grid=(pairs,),
        in_specs=[
            pl.BlockSpec(memory_space=pltpu.SMEM),
            vmem(),
            pl.BlockSpec((1, 2, table), lambda i: (i, 0, 0)),
            vmem(), vmem(), vmem(), vmem(),
        ],
        out_specs=[
            vmem(), vmem(), vmem(), vmem(),
            pl.BlockSpec((seqs, 2, total, total), lambda i: (0, i, 0, 0)),
        ],
        out_shape=[
            jax.ShapeDtypeStruct((parts, seqs, span, width), bf16),
            rows, rows, rows,
            jax.ShapeDtypeStruct((seqs, 2 * pairs, total, total), bf16),
        ],
        scratch_shapes=[pltpu.VMEM((2, span, table), f32)],
        compiler_params=params(),
        name="attention_forward",
    )(lens, tok, diag, gain, wq, wk, wv)


def mix_kernel(att_ref, tok_ref, slot_ref, wo_ref, gain_ref, hid_ref, send_ref, routed_ref):
    tokens, width = att_ref.shape
    slots = send_ref.shape[0]
    step = 256
    gain = gain_ref[...]

    def mix(i, carry):
        rows = pl.ds(pl.multiple_of(i * step, step), step)
        hidden = tok_ref[rows, :].astype(f32) + dot(att_ref[rows, :], wo_ref[...])
        hid_ref[rows, :] = hidden
        routed_ref[rows, :] = (hidden * inverse_rms(hidden) * gain).astype(bf16)
        return carry

    lax.fori_loop(0, tokens // step, mix, 0)

    def place(i, carry):
        rows = pl.ds(pl.multiple_of(i * step, step), step)
        ids = lax.broadcasted_iota(jnp.int32, (step, tokens), 0) + i * step
        pick = (ids == slot_ref[...]).astype(f32).astype(bf16)
        send_ref[rows, :] = dot(pick, routed_ref[...]).astype(bf16)
        return carry

    lax.fori_loop(0, slots // step, place, 0)


def mix(att, tok, slot_row, wo, gain, slots):
    tokens, width = att.shape
    return pl.pallas_call(
        mix_kernel,
        in_specs=[vmem()] * 5,
        out_specs=[vmem()] * 2,
        out_shape=[
            jax.ShapeDtypeStruct((tokens, width), f32),
            jax.ShapeDtypeStruct((slots, width), bf16),
        ],
        scratch_shapes=[pltpu.VMEM((tokens, width), bf16)],
        compiler_params=params(),
        name="mix",
    )(att, tok, slot_row, wo, gain)


def expert_kernel(
    experts, rows_ref, cot_ref, win_ref, wout_ref, wr_ref,
    res_ref, back_ref, gin_ref, gout_ref, grouter_ref,
    act_ref, pg_ref, push_ref, acc_res, acc_back,
):
    step_id = pl.program_id(0)
    chunk_rows = acc_res.shape[0]
    chunks = rows_ref.shape[0] // chunk_rows

    @pl.when(step_id < chunks)
    def _():
        expert_chunk(
            experts, step_id, rows_ref, cot_ref, win_ref, wout_ref, wr_ref, res_ref, back_ref,
            grouter_ref, act_ref, pg_ref, push_ref, acc_res, acc_back,
        )

    @pl.when(step_id >= chunks)
    def _():
        tile = gin_ref.shape[1]
        cols = pl.ds(pl.multiple_of((step_id - chunks) * tile, tile), tile)
        gin_ref[...] = dot(rows_ref[...], pg_ref[:, cols], TN).astype(bf16)
        gout_ref[...] = dot(act_ref[:, cols], push_ref[...], TN).astype(bf16)


def expert_chunk(
    experts, chunk, rows_ref, cot_ref, win_ref, wout_ref, wr_ref, res_ref, back_ref,
    grouter_ref, act_ref, pg_ref, push_ref, acc_res, acc_back,
):
    hidden_units = win_ref.shape[1]
    tile = 512
    chunk_rows = acc_res.shape[0]
    mine = lax.axis_index("wide")
    here = pl.ds(pl.multiple_of(chunk * chunk_rows, chunk_rows), chunk_rows)
    x = rows_ref[here, :]
    cot = cot_ref[here, :].astype(f32)
    lane = lax.broadcasted_iota(jnp.int32, (1, wr_ref.shape[1]), 1)
    logits = jnp.where(lane < experts, dot(x, wr_ref[...]), -1e30)
    raised = jnp.exp(logits - jnp.max(logits, axis=-1, keepdims=True))
    probs = raised * (1.0 / jnp.sum(raised, axis=-1, keepdims=True))
    hot = lane == mine
    gate = jnp.sum(jnp.where(hot, probs, 0.0), axis=-1, keepdims=True)
    push = (gate * cot).astype(bf16)
    push_ref[here, :] = push
    acc_res[...] = jnp.zeros_like(acc_res)
    acc_back[...] = jnp.zeros_like(acc_back)
    c0 = 0.7978845608028654
    c1 = c0 * 0.044715

    def units(t, carry):
        cols = pl.ds(pl.multiple_of(t * tile, tile), tile)
        pre = dot(x, win_ref[:, cols])
        ag = dot(push, wout_ref[cols, :], NT)
        sq = pre * pre
        th = jnp.tanh(pre * (c0 + c1 * sq))
        half = 0.5 + 0.5 * th
        act = (pre * half).astype(bf16)
        slope = half + pre * (0.5 - 0.5 * th * th) * (c0 + 3.0 * c1 * sq)
        pg = (ag * slope).astype(bf16)
        act_ref[here, cols] = act
        pg_ref[here, cols] = pg
        acc_res[...] += dot(act, wout_ref[cols, :])
        acc_back[...] += dot(pg, win_ref[:, cols], NT)
        return carry

    lax.fori_loop(0, hidden_units // tile, units, 0)
    result = acc_res[...].astype(bf16).astype(f32)
    res_ref[here, :] = (gate * result).astype(bf16)
    gate_grad = jnp.sum(cot * result, axis=-1, keepdims=True)
    logit_grad = probs * (jnp.where(hot, gate_grad, 0.0) - gate * gate_grad)
    logit_grad = logit_grad.astype(bf16)
    back = acc_back[...].astype(bf16).astype(f32) + dot(logit_grad, wr_ref[...], NT)
    back_ref[here, :] = back.astype(bf16)
    part = dot(x, logit_grad, TN)

    @pl.when(chunk == 0)
    def _():
        grouter_ref[...] = part

    @pl.when(chunk > 0)
    def _():
        grouter_ref[...] += part


def run_experts(rows, cot_rows, win, wout, wr, experts):
    count, width = rows.shape
    units = win.shape[1]
    chunks, tile = 4, 512
    step = count // chunks
    same = jax.ShapeDtypeStruct((count, width), bf16)
    return pl.pallas_call(
        functools.partial(expert_kernel, experts),
        grid=(chunks + units // tile,),
        in_specs=[vmem()] * 5,
        out_specs=[
            vmem(),
            vmem(),
            pl.BlockSpec((width, tile), lambda i: (0, jnp.maximum(i - chunks, 0))),
            pl.BlockSpec((tile, width), lambda i: (jnp.maximum(i - chunks, 0), 0)),
            vmem(),
        ],
        out_shape=[
            same,
            same,
            jax.ShapeDtypeStruct((width, units), bf16),
            jax.ShapeDtypeStruct((units, width), bf16),
            jax.ShapeDtypeStruct((width, wr.shape[1]), f32),
        ],
        scratch_shapes=[
            pltpu.VMEM((count, units), bf16),
            pltpu.VMEM((count, units), bf16),
            pltpu.VMEM((count, width), bf16),
            pltpu.VMEM((step, width), f32),
            pltpu.VMEM((step, width), f32),
        ],
        compiler_params=params(),
        name="experts",
    )(rows, cot_rows, win, wout, wr)


def hidden_back_kernel(
    back_ref, slot_ref, hid_ref, cot_ref, att_ref, wo_ref, gain_ref,
    hg_ref, ag_ref, gwo_ref, ggain_ref, branch_ref,
):
    tokens, width = hid_ref.shape
    slots = back_ref.shape[0]
    step = 256
    gain = gain_ref[...]
    ggain_ref[...] = jnp.zeros_like(ggain_ref)

    def pull(i, carry):
        rows = pl.ds(pl.multiple_of(i * step, step), step)
        ids = lax.broadcasted_iota(jnp.int32, (step, slots), 1)
        pick = (ids == slot_ref[rows, :]).astype(f32).astype(bf16)
        upstream = dot(pick, back_ref[...])
        hidden = hid_ref[rows, :]
        inv = inverse_rms(hidden)
        scaled = upstream * gain
        inner = jnp.mean(scaled * hidden, axis=-1, keepdims=True)
        grad = cot_ref[rows, :].astype(f32) + inv * scaled - hidden * (inv * inv * inv * inner)
        ggain_ref[...] += jnp.sum(upstream * hidden * inv, axis=0, keepdims=True)
        hg_ref[rows, :] = grad
        low = grad.astype(bf16)
        branch_ref[rows, :] = low
        ag_ref[rows, :] = dot(low, wo_ref[...], NT).astype(bf16)
        return carry

    lax.fori_loop(0, tokens // step, pull, 0)

    def weight(i, carry):
        cols = pl.ds(pl.multiple_of(i * 256, 256), 256)
        gwo_ref[:, cols] = dot(att_ref[...], branch_ref[:, cols], TN).astype(bf16)
        return carry

    lax.fori_loop(0, width // 256, weight, 0)


def hidden_back(back, slot_col, hid, cot, att, wo, gain):
    tokens, width = hid.shape
    return pl.pallas_call(
        hidden_back_kernel,
        in_specs=[vmem()] * 7,
        out_specs=[vmem()] * 4,
        out_shape=[
            jax.ShapeDtypeStruct((tokens, width), f32),
            jax.ShapeDtypeStruct((tokens, width), bf16),
            jax.ShapeDtypeStruct((width, width), bf16),
            jax.ShapeDtypeStruct((1, width), f32),
        ],
        scratch_shapes=[pltpu.VMEM((tokens, width), bf16)],
        compiler_params=params(),
        name="hidden_back",
    )(back, slot_col, hid, cot, att, wo, gain)


def attention_backward_kernel(
    ag_ref, p_ref, q_ref, k_ref, v_ref, tok_ref, gain_ref, wq_ref, wk_ref, wv_ref,
    gq_ref, gk_ref, gv_ref, part_ref, ggain_ref, diag_ref,
    dq_ref, dk_ref, dv_ref, strip_ref, normed_ref,
):
    pair = pl.program_id(0)
    parts, seqs, span, width = tok_ref.shape
    total = parts * span
    table = diag_ref.shape[-1]
    low, masks = half_masks(128)
    lanes = pl.ds(pl.multiple_of(pair * 128, 128), 128)
    strip_ref[...] = jnp.zeros_like(strip_ref)

    def one_sequence(s, carry):
        kp = k_ref[s, :, lanes]
        vp = v_ref[s, :, lanes]
        rows_all = pl.ds(pl.multiple_of(s * total, total), total)
        dk = [0.0, 0.0]
        dv = [0.0, 0.0]
        for block in range(parts // 2):
            rows = slice(block * 2 * span, (block + 1) * 2 * span)
            qp = q_ref[s, rows, lanes]
            gp = ag_ref[2 * block : 2 * block + 2, s, :, lanes].reshape(2 * span, 128)
            dq = None
            for hh in range(2):
                prob_low = p_ref[s, hh, rows, :]
                prob = prob_low.astype(f32)
                prob_grad = dot(gp * masks[hh], vp, NT)
                delta = jnp.sum(prob * prob_grad, axis=-1, keepdims=True)
                score_grad = prob * (prob_grad - delta)
                for r in range(2):
                    at = (parts - 1 - (2 * block + r)) * span
                    strip_ref[hh, :, at : at + total] += score_grad[r * span : (r + 1) * span]
                score_grad = score_grad.astype(bf16)
                part = dot(score_grad, kp)
                dq = part if hh == 0 else jnp.where(low, dq, part)
                dk[hh] = dk[hh] + dot(score_grad, qp, TN)
                dv[hh] = dv[hh] + dot(prob_low, gp, TN)
            at_rows = pl.ds(pl.multiple_of(s * total + block * 2 * span, 2 * span), 2 * span)
            dq_ref[at_rows, lanes] = dq.astype(bf16)
        dk_ref[rows_all, lanes] = jnp.where(low, dk[0], dk[1]).astype(bf16)
        dv_ref[rows_all, lanes] = jnp.where(low, dv[0], dv[1]).astype(bf16)
        return carry

    lax.fori_loop(0, seqs, one_sequence, 0)
    back = lax.broadcasted_iota(jnp.int32, (span, span), 0)
    flip = (back + lax.broadcasted_iota(jnp.int32, (span, span), 1) == span - 1).astype(f32)
    for hh in range(2):
        turned = lax.dot_general(
            flip, strip_ref[hh], NN, precision=lax.Precision.HIGHEST, preferred_element_type=f32
        )
        turned = pltpu.roll(turned, 0, 1, stride=1, stride_axis=0)
        diag_ref[0, hh : hh + 1, :] = jnp.sum(turned, axis=0, keepdims=True)

    @pl.when(pair == pl.num_programs(0) - 1)
    def _():
        gain = gain_ref[...]
        ggain_ref[...] = jnp.zeros_like(ggain_ref)

        def pull(step, carry):
            s, n = step // (parts // 2), step % (parts // 2)
            x = tok_ref[pl.ds(2 * n, 2), s].reshape(2 * span, width).astype(f32)
            inv = inverse_rms(x)
            rows = pl.ds(pl.multiple_of(step * 2 * span, 2 * span), 2 * span)
            normed_ref[rows, :] = (x * inv * gain).astype(bf16)
            upstream = dot(dq_ref[rows, :], wq_ref[...], NT)
            upstream += dot(dk_ref[rows, :], wk_ref[...], NT)
            upstream += dot(dv_ref[rows, :], wv_ref[...], NT)
            scaled = upstream * gain
            inner = jnp.mean(scaled * x, axis=-1, keepdims=True)
            grad = inv * scaled - x * (inv * inv * inv * inner)
            ggain_ref[...] += jnp.sum(upstream * x * inv, axis=0, keepdims=True)
            grad = grad.astype(bf16).reshape(2, span, width)
            part_ref[pl.ds(2 * n, 2), s] = grad
            return carry

        lax.fori_loop(0, seqs * (parts // 2), pull, 0)

        def weight(i, carry):
            cols = pl.ds(pl.multiple_of(i * 256, 256), 256)
            gq_ref[:, cols] = dot(normed_ref[...], dq_ref[:, cols], TN).astype(bf16)
            gk_ref[:, cols] = dot(normed_ref[...], dk_ref[:, cols], TN).astype(bf16)
            gv_ref[:, cols] = dot(normed_ref[...], dv_ref[:, cols], TN).astype(bf16)
            return carry

        lax.fori_loop(0, width // 256, weight, 0)


def attention_backward(ag, p, q, k, v, tok, gain, wq, wk, wv, table):
    parts, seqs, span, width = tok.shape
    total = parts * span
    pairs = p.shape[1] // 2
    square = jax.ShapeDtypeStruct((width, width), bf16)
    rows = pltpu.VMEM((seqs * total, width), bf16)
    return pl.pallas_call(
        attention_backward_kernel,
        grid=(pairs,),
        in_specs=[
            vmem(),
            pl.BlockSpec((seqs, 2, total, total), lambda i: (0, i, 0, 0)),
        ]
        + [vmem()] * 8,
        out_specs=[vmem()] * 5 + [pl.BlockSpec((1, 2, table), lambda i: (i, 0, 0))],
        out_shape=[
            square, square, square,
            jax.ShapeDtypeStruct((parts, seqs, span, width), bf16),
            jax.ShapeDtypeStruct((1, width), f32),
            jax.ShapeDtypeStruct((pairs, 2, table), f32),
        ],
        scratch_shapes=[rows, rows, rows, pltpu.VMEM((2, span, table), f32), rows],
        compiler_params=params(),
        name="attention_backward",
    )(ag, p, q, k, v, tok, gain, wq, wk, wv)


def finish_kernel(res_ref, slot_ref, hid_ref, out_ref):
    tokens, width = hid_ref.shape
    slots = res_ref.shape[0]
    step = 256

    def add(i, carry):
        rows = pl.ds(pl.multiple_of(i * step, step), step)
        ids = lax.broadcasted_iota(jnp.int32, (step, slots), 1)
        pick = (ids == slot_ref[rows, :]).astype(f32).astype(bf16)
        out_ref[rows, :] = hid_ref[rows, :] + dot(pick, res_ref[...])
        return carry

    lax.fori_loop(0, tokens // step, add, 0)


def finish(res, slot_col, hid):
    return pl.pallas_call(
        finish_kernel,
        in_specs=[vmem()] * 3,
        out_specs=vmem(),
        out_shape=jax.ShapeDtypeStruct(hid.shape, f32),
        compiler_params=params(),
        name="finish",
    )(res, slot_col, hid)


def body(
    tokens, lengths, routes, bucket_table, attn_gain, query_weight, key_weight, value_weight,
    output_weight, relative_bias, expert_gain, router_weight, experts_in, experts_out, cotangent,
):
    seq_count, span, width = tokens.shape
    narrow_n = lax.axis_size("narrow")
    wide_n = lax.axis_size("wide")
    seqs = seq_count // narrow_n
    heads = relative_bias.shape[1]
    buckets = relative_bias.shape[0]
    experts = router_weight.shape[1]
    tok_count = seq_count * span
    capacity = 5 * tok_count // (4 * experts)
    cap = -(-capacity // 16) * 16
    slots = experts * cap
    table = 2 * span * narrow_n
    gain_a = attn_gain.astype(f32).reshape(1, width)
    gain_e = expert_gain.astype(f32).reshape(1, width)
    router = jnp.pad(router_weight, ((0, 0), (0, -experts % 128)))

    def swap(array):
        return lax.all_to_all(array, "narrow", split_axis=0, concat_axis=0, tiled=True)

    def trade(array):
        array = array.reshape(wide_n, -1, width)
        return lax.all_to_all(array, "wide", split_axis=0, concat_axis=0, tiled=True).reshape(
            -1, width
        )

    table_ids = jnp.pad(bucket_table, (0, 1))
    offset_hot = (table_ids[None, :] == jnp.arange(buckets, dtype=jnp.int32)[:, None]).astype(bf16)
    diag = dot(relative_bias, offset_hot, TN).reshape(heads // 2, 2, table)
    route_ids = routes.reshape(tok_count)
    onehot = route_ids[:, None] == jnp.arange(experts, dtype=jnp.int32)[None, :]
    counts = jnp.cumsum(onehot.astype(jnp.int32), axis=0)
    position = jnp.sum(jnp.where(onehot, counts - 1, 0), axis=-1)
    slot = jnp.where(position < capacity, route_ids * cap + position, slots)
    slot_row, slot_col = slot.reshape(1, tok_count), slot.reshape(tok_count, 1)

    flat_cot = cotangent.reshape(tok_count, width)
    pick = (jnp.arange(slots, dtype=jnp.int32)[:, None] == slot_row).astype(bf16)
    cot_rows = trade(dot(pick, flat_cot).astype(bf16))

    tok_seq = swap(tokens).reshape(narrow_n, seqs, span, width)
    att_seq, q, k, v, probs = attention_forward(
        lengths, tok_seq, diag, gain_a, query_weight, key_weight, value_weight
    )
    attended = swap(att_seq.reshape(seq_count, span, width)).reshape(tok_count, width)
    flat_tok = tokens.reshape(tok_count, width)
    hidden, send_rows = mix(attended, flat_tok, slot_row, output_weight, gain_e, slots)
    rows = trade(send_rows)
    res, back, term_in, term_out, router_grad = run_experts(
        rows, cot_rows, experts_in[0], experts_out[0], router, experts
    )
    back_rows = trade(back)
    res_rows = trade(res)
    hidden_grad, att_grad, output_grad, gain_second = hidden_back(
        back_rows, slot_col, hidden, flat_cot, attended, output_weight, gain_e
    )
    layer_output = finish(res_rows, slot_col, hidden).reshape(seq_count, span, width)
    ag_seq = swap(att_grad.reshape(seq_count, span, width)).reshape(narrow_n, seqs, span, width)
    grad_query, grad_key, grad_value, part, gain_first, diag_grad = attention_backward(
        ag_seq, probs, q, k, v, tok_seq, gain_a, query_weight, key_weight, value_weight, table
    )
    part = swap(part.reshape(seq_count, span, width))
    input_grad = hidden_grad.reshape(seq_count, span, width) + part.astype(f32)
    relative_grad = lax.dot_general(
        offset_hot.astype(f32),
        diag_grad.reshape(heads, table),
        NT,
        precision=lax.Precision.HIGHEST,
        preferred_element_type=f32,
    )

    def scatter(array, dim=0):
        return lax.psum_scatter(
            array.astype(bf16), "narrow", scatter_dimension=dim, tiled=True
        ).astype(f32)

    grad_experts_in = scatter(term_in)[None]
    grad_experts_out = scatter(term_out)[None]
    shares = tuple(
        scatter(item)
        for item in (
            grad_query, grad_key, grad_value, output_grad, router_grad[:, :experts],
            relative_grad, gain_first[0], gain_second[0],
        )
    )
    totals = lax.psum(shares, "wide")
    return (
        layer_output,
        input_grad,
        totals[6],
        totals[0],
        totals[1],
        totals[2],
        totals[3],
        totals[5],
        totals[7],
        totals[4],
        grad_experts_in,
        grad_experts_out,
    )


def solution(mesh):
    token = P("wide", "narrow", None)
    expert = P("wide", None, None)
    row, vector = P("narrow", None), P("narrow")
    return jax.shard_map(
        body,
        mesh=mesh,
        in_specs=(token, P("wide"), token) + (P(),) * 9 + (expert, expert, token),
        out_specs=(
            token, token, vector, row, row, row, row, row, vector, row,
            P("wide", "narrow", None), P("wide", "narrow", None),
        ),
        check_vma=False,
    )
```

time: 1420 us -> 605 us (0.43)
  local copies, waits for them, and re-layouts: 707 us -> 11.2 us
  waiting for transfers between devices: 345 us -> 157 us
  Pallas kernels: 0 us -> 175 us
  matrix products: 163 us -> 4.01 us
  blocking collectives: 112 us -> 201 us
  other arithmetic: 46.5 us -> 13.9 us
    gather x6 -> x0, local copies, waits for them, and re-layouts: 508 us -> none  [the longest x2 261 us: body(): bucket_table[key_cols[None, :] - query_rows[:, None] + seq_len - 1]]
    reduce_scatter x6 -> x7, waiting for transfers between devices: 187 us -> 0.04 us  [scatter(): lax.psum_scatter(array.astype(bf16), 'narrow', scatter_dimension=dim, til...]
    pallas_call x0 -> x6, Pallas kernels: none -> 175 us  [the longest x1 59.7 us: run_experts(): pl.pallas_call(functools.partial(expert_kernel, experts), grid=(chunks +...]
    dot_general x78 -> x3, matrix products: 163 us -> 4.01 us  [the longest x2 3.85 us: dot(): return lax.dot_general(a, b, dims, preferred_element_type=f32)]
    all_to_all x0 -> x2, blocking collectives: none -> 79.9 us  [the longest x1 49.1 us: trade(): lax.all_to_all(array, 'wide', split_axis=0, concat_axis=0, tiled=True)]
    unnamed x97 -> x41, local copies, waits for them, and re-layouts: 66.5 us -> 7.23 us
    dynamic_slice x72 -> x0, local copies, waits for them, and re-layouts: 57.6 us -> none  [body(): lax.map(forward_one, (queries, keys_all, values_all, key_valid))]
    unnamed x14 -> x7, waiting for transfers between devices: 52.3 us -> 2.31 us
  transfers between devices with their start and end apart: 15 -> 13, of which waited for: 13 -> 5; matrix products, arithmetic and copies ran while one was open for 49% -> 3% of each run, Pallas kernels for 0% -> 13%
where the time goes in v1:
time: 605 us; the launch traced here: 604 us
  blocking collectives  201 us (33%)
  Pallas kernels  175 us (29%)
  waiting for transfers between devices  157 us (26%)
  starting transfers between devices  26.9 us (4%)
  between operations  15.7 us (3%)
  other arithmetic  13.9 us (2%)
  local copies, waits for them, and re-layouts  11.2 us (2%)
    all_to_all x3, waiting for transfers between devices, trade(): lax.all_to_all(array, 'wide', split_axis=0, concat_axis=0, tiled=True)  122 us
    psum x1, blocking collectives, body(): totals = lax.psum(shares, 'wide')  101 us
    pallas_call x1, Pallas kernels, run_experts(): pl.pallas_call(functools.partial(expert_kernel, experts), grid=(chunks +...  59.7 us
    pallas_call x1, Pallas kernels, attention_backward(): pl.pallas_call(attention_backward_kernel, grid=(pairs,), in_specs=[vmem()...  49.3 us
    all_to_all x1, blocking collectives, trade(): lax.all_to_all(array, 'wide', split_axis=0, concat_axis=0, tiled=True)  49.1 us
    pallas_call x1, Pallas kernels, attention_forward(): pl.pallas_call(attention_forward_kernel, grid=(pairs,), in_specs=[pl.Bloc...  35.2 us
    all_to_all x3, waiting for transfers between devices, swap(): lax.all_to_all(array, 'narrow', split_axis=0, concat_axis=0, tiled=True)  32.2 us
    all_to_all x1, blocking collectives, swap(): lax.all_to_all(array, 'narrow', split_axis=0, concat_axis=0, tiled=True)  30.8 us
  transfers between devices with their start and end apart: 13, of which 5 were waited for; matrix products, arithmetic and copies ran while one was open for 3% of the time, Pallas kernels for 13%

profile of v1, /device:TPU:0, one launch (start us, length us, event | category | flops | bytes accessed | tf_op | source)
XLA Modules:
  0.0 604.4 jit_solution(1210601239801539448)
XLA Ops:
  7.2 4.4 all-to-all-start
  13.0 18.7 %all-to-all-done = bf16[8,128,768]{2,1,0:T(8,128)(2,1)S(1)} async-done(((bf16[8,128,768]{2,1,0:T(8,128)(2,1)}), bf16[8,128,768]{2,1,0:T(8,128)(2,1)S(1)}, u32[]{:S(2)}, u32[]{:S(2)}) %all-to-all-start) | async-done | bytes 1572896 | tf_op jit(solution)/shard_map/all_to_all | solution.py:513
  32.9 35.2 %attention_forward.1 = (bf16[4,2,128,768]{3,2,1,0:T(8,128)(2,1)}, bf16[2,512,768]{2,1,0:T(8,128)(2,1)}, bf16[2,512,768]{2,1,0:T(8,128)(2,1)}, bf16[2,512,768]{2,1,0:T(8,128)(2,1)}, bf16[2,12,512,512]{3,2,1,0:T(8,128)(2,1)}) custom-call(s32[8]{0:T(128)} %lens_ref.1, bf16[4,2,128,768]{3,2,1,0:T(8,128)(2,1)} %bitcast.54, f32[6,2,1024]{2,1,0:T(2,128)} %reshape.171.diag_ref, ...), custom_call_target="tpu_custom_call" | custom-call | tf_op jit(solution)/shard_map/attention_forward/pallas_call | solution.py:112
  68.1 3.7 all-to-all-start.1
  74.7 3.7 fusion.1
  78.4 13.5 %all-to-all-done.1 = bf16[8,128,768]{2,1,0:T(8,128)(2,1)S(1)} async-done(((bf16[8,128,768]{2,1,0:T(8,128)(2,1)}), bf16[8,128,768]{2,1,0:T(8,128)(2,1)S(1)}, u32[]{:S(2)}, u32[]{:S(2)}) %all-to-all-start.1) | async-done | bytes 1572896 | tf_op jit(solution)/shard_map/all_to_all | solution.py:513
  93.0 6.6 %all-to-all-start.3 = ((bf16[8,160,768]{2,1,0:T(8,128)(2,1)}), bf16[8,160,768]{2,1,0:T(8,128)(2,1)S(1)}, u32[]{:S(2)}, u32[]{:S(2)}) async-start(bf16[8,160,768]{2,1,0:T(8,128)(2,1)} %bitcast.69), calls=%async_computation.3 | async-start | bytes 3932160 | tf_op jit(solution)/shard_map/all_to_all | solution.py:517
  100.8 9.3 %mix.1 = (f32[1024,768]{1,0:T(8,128)}, bf16[1280,768]{1,0:T(8,128)(2,1)}) custom-call(bf16[1024,768]{1,0:T(8,128)(2,1)} %bitcast.56, bf16[1024,768]{1,0:T(8,128)(2,1)} %bitcast.61, s32[1,1024]{1,0:T(1,128)} %compare_select_fusion.slot_ref, bf16[768,768]{1,0:T(8,128)(2,1)} %wo_ref.3, f32[1,768]{1,0:T(1,128)} %reshape.198.gain_ref), custom_call_target="tpu_custom_call" | custom-call | tf_op jit(solution)/shard_map/mix/pallas_call | solution.py:163
  110.1 34.8 %all-to-all-done.3 = bf16[8,160,768]{2,1,0:T(8,128)(2,1)S(1)} async-done(((bf16[8,160,768]{2,1,0:T(8,128)(2,1)}), bf16[8,160,768]{2,1,0:T(8,128)(2,1)S(1)}, u32[]{:S(2)}, u32[]{:S(2)}) %all-to-all-start.3) | async-done | bytes 1966112 | tf_op jit(solution)/shard_map/all_to_all | solution.py:517
  146.1 4.4 all-to-all-start.2
  151.4 44.1 %all-to-all-done.2 = bf16[8,160,768]{2,1,0:T(8,128)(2,1)} async-done(((bf16[8,160,768]{2,1,0:T(8,128)(2,1)}), bf16[8,160,768]{2,1,0:T(8,128)(2,1)}, u32[]{:S(2)}, u32[]{:S(2)}) %all-to-all-start.2) | async-done | bytes 1966112 | tf_op jit(solution)/shard_map/all_to_all | solution.py:517
  195.5 59.7 %experts.1 = (bf16[1280,768]{1,0:T(8,128)(2,1)}, bf16[1280,768]{1,0:T(8,128)(2,1)}, bf16[768,3072]{1,0:T(8,128)(2,1)}, bf16[3072,768]{1,0:T(8,128)(2,1)}, f32[768,128]{1,0:T(8,128)}) custom-call(bf16[1280,768]{1,0:T(8,128)(2,1)} %bitcast.12.rows_ref, bf16[1280,768]{1,0:T(8,128)(2,1)} %bitcast.58, bf16[768,3072]{1,0:T(8,128)(2,1)} %bitcast.63, ...), custom_call_target="tpu_custom_call" | custom-call | tf_op jit(solution)/shard_map/experts/pallas_call | solution.py:266
  255.3 3.8 all-to-all-start.5
  261.3 43.3 %all-to-all-done.5 = bf16[8,160,768]{2,1,0:T(8,128)(2,1)S(1)} async-done(((bf16[8,160,768]{2,1,0:T(8,128)(2,1)}), bf16[8,160,768]{2,1,0:T(8,128)(2,1)S(1)}, u32[]{:S(2)}, u32[]{:S(2)}) %all-to-all-start.5) | async-done | bytes 1966112 | tf_op jit(solution)/shard_map/all_to_all | solution.py:517
  305.9 14.1 %hidden_back.1 = (f32[1024,768]{1,0:T(8,128)}, bf16[1024,768]{1,0:T(8,128)(2,1)}, bf16[768,768]{1,0:T(8,128)(2,1)}, f32[1,768]{1,0:T(1,128)}) custom-call(bf16[1280,768]{1,0:T(8,128)(2,1)} %bitcast.59, s32[1024,1]{1,0:T(8,128)} %add_select_fusion.slot_ref, f32[1024,768]{1,0:T(8,128)} %get-tuple-element.37.hid_ref, bf16[1024,768]{1,0:T(8,128)(2,1)} %bitcast.73, ...), custom_call_target="tpu_custom_call" | custom-call | tf_op jit(solution)/shard_map/hidden_back/pallas_call | solution.py:335
  320.1 30.8 %all_to_all.40 = bf16[8,128,768]{2,1,0:T(8,128)(2,1)} all-to-all(bf16[8,128,768]{2,1,0:T(8,128)(2,1)} %bitcast.72), channel_id=1, replica_groups=mesh['wide'=8,'narrow'=4] {'narrow'}, dimensions={0} | all-to-all | bytes 3145728 | tf_op jit(solution)/shard_map/all_to_all | solution.py:513
  350.9 49.3 %attention_backward.1 = (bf16[768,768]{1,0:T(8,128)(2,1)}, bf16[768,768]{1,0:T(8,128)(2,1)}, bf16[768,768]{1,0:T(8,128)(2,1)}, bf16[4,2,128,768]{3,2,1,0:T(8,128...) custom-call(bf16[4,2,128,768]{3,2,1,0:T(8,128)(2,1)} %bitcast.62, bf16[2,12,512,512]{3,2,1,0:T(8,128)(2,1)} %get-tuple-element.41.p_ref, ...), custom_call_target="tpu_custom_call" | custom-call | tf_op jit(solution)/shard_map/attention_backward/pallas_call | solution.py:445
  403.6 49.1 %all_to_all.41 = bf16[8,160,768]{2,1,0:T(8,128)(2,1)} all-to-all(bf16[8,160,768]{2,1,0:T(8,128)(2,1)S(1)} %bitcast.67), channel_id=1, replica_groups=mesh['wide'=8,'narrow'=4] {'wide'}, dimensions={0} | all-to-all | bytes 3932160 | tf_op jit(solution)/shard_map/all_to_all | solution.py:517
  452.6 3.7 all-to-all-start.7
  458.3 7.7 %finish.1 = f32[1024,768]{1,0:T(8,128)} custom-call(bf16[1280,768]{1,0:T(8,128)(2,1)} %bitcast.60, s32[1024,1]{1,0:T(8,128)} %add_select_fusion.slot_ref, f32[1024,768]{1,0:T(8,128)} %get-tuple-element.37.hid_ref), custom_call_target="tpu_custom_call" | custom-call | tf_op jit(solution)/shard_map/finish/pallas_call | solution.py:482
  466.2 19.3 %all-reduce.6 = (bf16[768]{0:T(1024)(128)(2,1)S(1)}, bf16[32,12]{1,0:T(8,128)(2,1)S(1)}, bf16[768]{0:T(1024)(128)(2,1)S(1)}) all-reduce(bf16[768]{0:T(1024)(128)(2,1)S(1)} %convert_reduce_fusion.1, bf16[32,12]{1,0:T(8,128)(2,1)S(1)} %convolution_convert_fusion, ...), channel_id=2, replica_groups=mesh['wide'=8,'narrow'=4] {'narrow'}, use_global_device_ids=true, to_apply=%region_3.4.clone | all-reduce | flops 1920 | bytes 7680
  485.6 4.0 convert_add_fusion
  489.7 101.5 %all-reduce.8 = (f32[192]{0:T(256)}, f32[192,768]{1,0:T(8,128)}, f32[192,768]{1,0:T(8,128)}, f32[192,768]{1,0:T(8,128)}, f32[192,768]{1,0:T(8,128)}, /*index=5*/...) all-reduce(f32[192]{0:T(256)S(1)} %get-tuple-element.104, ...), channel_id=1, replica_groups=mesh['wide'=8,'narrow'=4] {'wide'}, use_global_device_ids=true, to_apply=%region_4.5 | all-reduce | flops 591840 | bytes 3552000 | tf_op jit(solution)/shard_map/psum | solution.py:580
  594.7 2.9 bitcast_convert_fusion.1
  (89 shorter events, 21.3 us)
Async XLA Ops:
  7.2 5.0 copy-start
  7.2 4.4 copy-start.16
  7.2 4.9 copy-start.13
  7.2 24.4 %all-to-all-start = ((bf16[8,128,768]{2,1,0:T(8,128)(2,1)}), bf16[8,128,768]{2,1,0:T(8,128)(2,1)S(1)}, u32[]{:S(2)}, u32[]{:S(2)}) async-start(bf16[8,128,768]{2,1,0:T(8,128)(2,1)} %param.15), calls=%async_computation | async-start | bytes 3145728 | tf_op jit(solution)/shard_map/all_to_all | solution.py:513
  68.1 6.6 %copy-start.7 = (bf16[8,128,768]{2,1,0:T(8,128)(2,1)S(1)}, bf16[8,128,768]{2,1,0:T(8,128)(2,1)}, u32[]{:S(2)}) copy-start(bf16[8,128,768]{2,1,0:T(8,128)(2,1)} %param.29) | copy-start | bytes 4718596
  68.1 23.8 %all-to-all-start.1 = ((bf16[8,128,768]{2,1,0:T(8,128)(2,1)}), bf16[8,128,768]{2,1,0:T(8,128)(2,1)S(1)}, u32[]{:S(2)}, u32[]{:S(2)}) async-start(bf16[8,128,768]{2,1,0:T(8,128)(2,1)} %bitcast.71), calls=%async_computation.1 | async-start | bytes 3145728 | tf_op jit(solution)/shard_map/all_to_all | solution.py:513
  91.9 7.8 %copy-start.17 = (bf16[768]{0:T(1024)(128)(2,1)S(1)}, bf16[768]{0:T(1024)(128)(2,1)}, u32[]{:S(2)}) copy-start(bf16[768]{0:T(1024)(128)(2,1)} %param.25) | copy-start | bytes 4612
  93.0 51.8 %all-to-all-start.3 = ((bf16[8,160,768]{2,1,0:T(8,128)(2,1)}), bf16[8,160,768]{2,1,0:T(8,128)(2,1)S(1)}, u32[]{:S(2)}, u32[]{:S(2)}) async-start(bf16[8,160,768]{2,1,0:T(8,128)(2,1)} %bitcast.69), calls=%async_computation.3 | async-start | bytes 3932160 | tf_op jit(solution)/shard_map/all_to_all | solution.py:517
  144.9 5.6 copy-start.12
  146.1 49.4 %all-to-all-start.2 = ((bf16[8,160,768]{2,1,0:T(8,128)(2,1)}), bf16[8,160,768]{2,1,0:T(8,128)(2,1)}, u32[]{:S(2)}, u32[]{:S(2)}) async-start(bf16[8,160,768]{2,1,0:T(8,128)(2,1)} %bitcast.70), calls=%async_computation.2 | async-start | bytes 3932160 | tf_op jit(solution)/shard_map/all_to_all | solution.py:517
  255.3 4.5 copy-start.8
  255.3 49.4 %all-to-all-start.5 = ((bf16[8,160,768]{2,1,0:T(8,128)(2,1)}), bf16[8,160,768]{2,1,0:T(8,128)(2,1)S(1)}, u32[]{:S(2)}, u32[]{:S(2)}) async-start(bf16[8,160,768]{2,1,0:T(8,128)(2,1)} %bitcast.68), calls=%async_computation.5 | async-start | bytes 3932160 | tf_op jit(solution)/shard_map/all_to_all | solution.py:517
  259.0 199.2 %reduce-scatter.16.cloned.1.call-start = ((), (), s32[]{:S(2)}) async-start(), calls=%async_computation.19 | async-start | bytes 245760 | tf_op jit(solution)/shard_map/reduce_scatter | solution.py:567
  260.4 229.2 %reduce-scatter.14.cloned.1.call-start = ((), (), s32[]{:S(2)}) async-start(), calls=%async_computation.18 | async-start | bytes 1474560 | tf_op jit(solution)/shard_map/reduce_scatter | solution.py:567
  320.0 169.6 %reduce-scatter.8.cloned.1.call-start = ((), (), s32[]{:S(2)}) async-start(), calls=%async_computation.15 | async-start | bytes 1474560 | tf_op jit(solution)/shard_map/reduce_scatter | solution.py:567
  400.2 89.4 %reduce-scatter.10.cloned.1.call-start = ((), (), s32[]{:S(2)}) async-start(), calls=%async_computation.16 | async-start | bytes 1474560 | tf_op jit(solution)/shard_map/reduce_scatter | solution.py:567
  400.8 88.8 %reduce-scatter.12.cloned.1.call-start = ((), (), s32[]{:S(2)}) async-start(), calls=%async_computation.17 | async-start | bytes 1474560 | tf_op jit(solution)/shard_map/reduce_scatter | solution.py:567
  401.4 190.4 %reduce-scatter.20.cloned.1.call-start = ((), (), s32[]{:S(2)}) async-start(), calls=%async_computation.21 | async-start | bytes 5898240 | tf_op jit(solution)/shard_map/reduce_scatter | solution.py:567
  402.0 192.7 %reduce-scatter.18.cloned.1.call-start = ((), (), s32[]{:S(2)}) async-start(), calls=%async_computation.20 | async-start | bytes 5898240 | tf_op jit(solution)/shard_map/reduce_scatter | solution.py:567
  452.6 33.0 %all-to-all-start.7 = ((bf16[8,128,768]{2,1,0:T(8,128)(2,1)}), bf16[8,128,768]{2,1,0:T(8,128)(2,1)S(1)}, u32[]{:S(2)}, u32[]{:S(2)}) async-start(bf16[8,128,768]{2,1,0:T(8,128)(2,1)} %bitcast.28), calls=%async_computation.7 | async-start | bytes 3145728 | tf_op jit(solution)/shard_map/all_to_all | solution.py:513
  458.3 7.7 %copy-start.14 = (f32[1,768]{1,0:T(1,128)S(1)}, f32[1,768]{1,0:T(1,128)}, u32[]{:S(2)}) copy-start(f32[1,768]{1,0:T(1,128)} %get-tuple-element.52) | copy-start | bytes 9220
  458.3 7.7 %copy-start.11 = (f32[6,2,1024]{2,1,0:T(2,128)S(1)}, f32[6,2,1024]{2,1,0:T(2,128)}, u32[]{:S(2)}) copy-start(f32[6,2,1024]{2,1,0:T(2,128)} %get-tuple-element.51) | copy-start | bytes 147460
  458.3 7.8 %copy-start.15 = (f32[1,768]{1,0:T(1,128)S(1)}, f32[1,768]{1,0:T(1,128)}, u32[]{:S(2)}) copy-start(f32[1,768]{1,0:T(1,128)} %get-tuple-element.46) | copy-start | bytes 9220
  591.8 5.8 copy-start.1
  (8 other events, 17.9 us)
Sparse Core Ops, SparseCore 0:
  262.9 20.2 reduce-scatter.15
  320.2 30.4 reduce-scatter.13
  400.3 23.7 reduce-scatter.7
  426.6 25.7 reduce-scatter.9
  454.9 28.8 reduce-scatter.11
  486.2 45.5 reduce-scatter.19
  534.6 47.8 reduce-scatter.17

commit v2 on v1

v2 whole, which is shorter than its diff:
```python
import functools

import jax
import jax.numpy as jnp
from jax import lax
from jax.experimental import pallas as pl
from jax.experimental.pallas import tpu as pltpu
from jax.sharding import PartitionSpec as P

f32, bf16 = jnp.float32, jnp.bfloat16
epsilon = 1e-06
VMEM_BYTES = 60 * 1024 * 1024
NN = (((1,), (0,)), ((), ()))
NT = (((1,), (1,)), ((), ()))
TN = (((0,), (0,)), ((), ()))


def dot(a, b, dims=NN):
    return lax.dot_general(a, b, dims, preferred_element_type=f32)


def vmem():
    return pl.BlockSpec(memory_space=pltpu.VMEM)


def params(**kw):
    return pltpu.CompilerParams(vmem_limit_bytes=VMEM_BYTES, **kw)


def inverse_rms(field):
    return lax.rsqrt(jnp.mean(field * field, axis=-1, keepdims=True) + epsilon)


def half_masks(pair_width):
    lane = lax.broadcasted_iota(jnp.int32, (1, pair_width), 1)
    low = lane < pair_width // 2
    return low, (low.astype(f32).astype(bf16), (~low).astype(f32).astype(bf16))


MESH = pl.DeviceIdType.MESH
LOG2E = 1.4426950408889634


def hbm():
    return pl.BlockSpec(memory_space=pl.ANY)


def flipped(me, k, size):
    out, bit = me, 1
    while bit < size:
        out = out + ((k // bit) % 2) * (bit - 2 * bit * ((me // bit) % 2))
        bit *= 2
    return out


def remote(src, dst, sems, k, axis, peer):
    return pltpu.make_async_remote_copy(
        src_ref=src,
        dst_ref=dst,
        send_sem=sems.at[0, k],
        recv_sem=sems.at[1, k],
        device_id={axis: peer},
        device_id_type=MESH,
    )


def enter(narrow_n, wide_n):
    barrier = pltpu.get_barrier_semaphore()
    count = 0
    for axis, size in (("narrow", narrow_n), ("wide", wide_n)):
        if size > 1:
            me = lax.axis_index(axis)

            def greet(k, carry, axis=axis, size=size, me=me):
                pl.semaphore_signal(
                    barrier, inc=1, device_id={axis: flipped(me, k, size)}, device_id_type=MESH
                )
                return carry

            lax.fori_loop(1, size, greet, 0)
            count += size - 1
    pl.semaphore_wait(barrier, count)


def expert_pick(expert, cap, slot_row):
    ids = lax.broadcasted_iota(jnp.int32, (cap, slot_row.shape[1]), 0) + expert * cap
    return (ids == slot_row).astype(f32).astype(bf16)


def forward_kernel(
    wide_n, lens_ref, tok_any, cot_ref, slot_ref, diag_ref, gain_a_ref, gain_e_ref,
    wq_ref, wk_ref, wv_ref, wo_ref,
    tokseq_any, attseq_any, att_any, hid_any, routed_any, cotrows_any, q_any, k_any, v_any, invl_any, p_any,
    tokbuf, tokpos, q_ref, k_ref, v_ref, invl_ref, attseq, attpos, hid_ref, routed_ref, cotsend,
    strip_ref, pbuf, vext, kext, toksem, attsem, cotsem, psem, outsem,
):
    parts, seqs, span, width = tokbuf.shape
    total = parts * span
    pairs, _, table = diag_ref.shape
    cap = cotsend.shape[1]
    n = lax.axis_index("narrow")
    w = lax.axis_index("wide")
    own = pltpu.make_async_copy(tok_any.at[n], tokbuf.at[n], outsem.at[0])
    own.start()
    position = pltpu.make_async_copy(tok_any, tokpos, outsem.at[1])
    position.start()
    enter(parts, wide_n)

    def tok_copy(k):
        peer = flipped(n, k, parts)
        return remote(tok_any.at[peer], tokbuf.at[n], toksem, k, "narrow", peer)

    for k in range(parts - 1, 0, -1):
        tok_copy(k).start()

    def cot_copy(k):
        peer = flipped(w, k, wide_n)
        return remote(cotsend.at[k], cotrows_any.at[k], cotsem, k, "wide", peer)

    def cot_block(k):
        pick = expert_pick(flipped(w, k, wide_n), cap, slot_ref[...])
        cotsend[k] = dot(pick, cot_ref[...]).astype(bf16)

    def cot_step(i, carry):
        k = wide_n - 1 - i
        cot_block(k)
        cot_copy(k).start()
        return carry

    lax.fori_loop(0, wide_n - 1, cot_step, 0)
    cot_block(0)
    cot_own = pltpu.make_async_copy(cotsend.at[0], cotrows_any.at[0], outsem.at[2])
    cot_own.start()

    gain = gain_a_ref[...]
    own.wait()
    for k in range(parts):
        src = flipped(n, k, parts)
        if k > 0:
            tok_copy(k).wait_recv()
        x = tokbuf[src].reshape(seqs * span, width).astype(f32)
        normed = (x * inverse_rms(x) * gain).astype(bf16)
        shape = (seqs, span, width)
        q_ref[src] = (dot(normed, wq_ref[...]) * LOG2E).astype(bf16).reshape(shape)
        k_ref[src] = dot(normed, wk_ref[...]).astype(bf16).reshape(shape)
        v_ref[src] = dot(normed, wv_ref[...]).astype(bf16).reshape(shape)
    outs = [
        pltpu.make_async_copy(a, b, outsem.at[i])
        for a, b, i in (
            (tokbuf, tokseq_any, 3), (q_ref, q_any, 4), (k_ref, k_any, 5), (v_ref, v_any, 6),
        )
    ]
    for copy in outs:
        copy.start()

    low, masks = half_masks(128)
    lane = lax.broadcasted_iota(jnp.int32, (1, 128), 1)
    hot = [(lane == 64).astype(f32).astype(bf16), (lane == 0).astype(f32).astype(bf16)]
    for hh in range(2):
        ones = jnp.broadcast_to(masks[hh], (total, 128))
        vext[hh * total : (hh + 1) * total, 128:] = ones

    def att_copy(k, lanes):
        peer = flipped(n, k, parts)
        return remote(
            attseq.at[peer, :, :, lanes], attpos.at[n, :, :, lanes], attsem, k, "narrow", peer
        )

    def one_pair(pair, carry):
        lanes = pl.ds(pl.multiple_of(pair * 128, 128), 128)
        for hh in range(2):
            row = diag_ref[pair, hh : hh + 1, :]
            strip_ref[hh] = pltpu.roll(
                jnp.broadcast_to(row, (span, table)), table - span + 1, 1, stride=1, stride_axis=0
            )

        def one_sequence(s, inner):
            vp = v_ref[:, s, :, lanes].reshape(total, 128)
            kp = k_ref[:, s, :, lanes].reshape(total, 128).astype(f32)
            ids = lax.broadcasted_iota(jnp.int32, (total, 128), 0)
            push = jnp.where(ids < lens_ref[n * seqs + s], 0.0, -1e30)
            for hh in range(2):
                vext[hh * total : (hh + 1) * total, :128] = vp * masks[hh]
                kext[hh] = jnp.where(lane == 64 - 64 * hh, push, kp).astype(bf16)

            @pl.when(pair > 0)
            def _():
                pltpu.make_async_copy(pbuf.at[s], p_any.at[pair, s], psem.at[s]).wait()

            for block in range(parts // 2):
                rows = slice(block * 2 * span, (block + 1) * 2 * span)
                both = slice(2 * block, 2 * block + 2)
                qp = q_ref[both, s, :, lanes].reshape(2 * span, 128)
                for hh in range(2):
                    bias = jnp.concatenate(
                        [
                            strip_ref[hh, :, (parts - 1 - r) * span : (parts - 1 - r) * span + total]
                            for r in (2 * block, 2 * block + 1)
                        ],
                        axis=0,
                    )
                    scores = dot(qp * masks[hh] + hot[hh], kext[hh], NT) + bias
                    raised = jnp.exp2(scores - jnp.max(scores, axis=-1, keepdims=True))
                    pbuf[s, rows, hh * total : (hh + 1) * total] = raised.astype(bf16)
                mixed = dot(pbuf[s, rows, :], vext[...])
                inv = 1.0 / mixed[:, 128:]
                invl_ref[both, s, :, lanes] = inv.reshape(2, span, 128)
                attseq[both, s, :, lanes] = (mixed[:, :128] * inv).astype(bf16).reshape(2, span, 128)
            pltpu.make_async_copy(pbuf.at[s], p_any.at[pair, s], psem.at[s]).start()
            return inner

        lax.fori_loop(0, seqs, one_sequence, 0)
        for k in range(parts - 1, 0, -1):
            att_copy(k, lanes).start()
        return carry

    lax.fori_loop(0, pairs, one_pair, 0)
    copy = pltpu.make_async_copy(invl_ref, invl_any, outsem.at[7])
    copy.start()
    outs.append(copy)
    position.wait()
    gain = gain_e_ref[...]
    for k in range(parts):
        src = flipped(n, k, parts)
        if k > 0:
            att_copy(k, slice(None)).wait_recv()
            att = attpos[src].reshape(seqs * span, width)
        else:
            attpos[src] = attseq[src]
            att = attseq[src].reshape(seqs * span, width)
        rows = pl.ds(pl.multiple_of(src * seqs * span, seqs * span), seqs * span)
        hidden = tokpos[src].reshape(seqs * span, width).astype(f32) + dot(att, wo_ref[...])
        hid_ref[rows, :] = hidden
        routed_ref[rows, :] = (hidden * inverse_rms(hidden) * gain).astype(bf16)
    for a, b, i in ((attpos, att_any, 8), (hid_ref, hid_any, 9), (routed_ref, routed_any, 10),
                    (attseq, attseq_any, 11)):
        copy = pltpu.make_async_copy(a, b, outsem.at[i])
        copy.start()
        outs.append(copy)
    for k in range(1, parts):
        tok_copy(k).wait_send()
        att_copy(k, slice(None)).wait_send()
    for s in range(seqs):
        pltpu.make_async_copy(pbuf.at[s], p_any.at[0, s], psem.at[s]).wait()
    cot_own.wait()

    def cot_wait(k, carry):
        cot_copy(k).wait()
        return carry

    lax.fori_loop(1, wide_n, cot_wait, 0)
    for copy in outs:
        copy.wait()


def forward(lens, tok, cot, slot_row, diag, gain_a, gain_e, wq, wk, wv, wo, wide_n, cap):
    parts, seqs, span, width = tok.shape
    pairs, _, table = diag.shape
    total = parts * span
    tokens = parts * seqs * span
    quad = (parts, seqs, span, width)
    shapes = [
        (quad, bf16), (quad, bf16), (quad, bf16), ((tokens, width), f32), ((tokens, width), bf16),
        ((wide_n, cap, width), bf16), (quad, bf16), (quad, bf16), (quad, bf16), (quad, f32),
        ((pairs, seqs, total, 2 * total), bf16),
    ]
    return pl.pallas_call(
        functools.partial(forward_kernel, wide_n),
        in_specs=[pl.BlockSpec(memory_space=pltpu.SMEM), hbm()] + [vmem()] * 9,
        out_specs=[hbm()] * len(shapes),
        out_shape=[jax.ShapeDtypeStruct(*item) for item in shapes],
        scratch_shapes=[
            pltpu.VMEM(quad, bf16),
            pltpu.VMEM(quad, bf16),
            pltpu.VMEM(quad, bf16),
            pltpu.VMEM(quad, bf16),
            pltpu.VMEM(quad, bf16),
            pltpu.VMEM(quad, f32),
            pltpu.VMEM(quad, bf16),
            pltpu.VMEM(quad, bf16),
            pltpu.VMEM((tokens, width), f32),
            pltpu.VMEM((tokens, width), bf16),
            pltpu.VMEM((wide_n, cap, width), bf16),
            pltpu.VMEM((2, span, table), f32),
            pltpu.VMEM((seqs, total, 2 * total), bf16),
            pltpu.VMEM((2 * total, 256), bf16),
            pltpu.VMEM((2, total, 128), bf16),
            pltpu.SemaphoreType.DMA((2, parts)),
            pltpu.SemaphoreType.DMA((2, parts)),
            pltpu.SemaphoreType.DMA((2, wide_n)),
            pltpu.SemaphoreType.DMA((seqs,)),
            pltpu.SemaphoreType.DMA((12,)),
        ],
        compiler_params=params(collective_id=1, has_side_effects=True),
        name="forward",
    )(lens, tok, cot, slot_row, diag, gain_a, gain_e, wq, wk, wv, wo)


def expert_kernel(
    experts, chunks, routed_ref, slot_ref, wr_ref, cot_any, win_any, wout_any,
    res_any, back_any, gin_any, gout_any, grouter_ref,
    send_ref, recv_ref, cot_ref, push_ref, win_ref, wout_ref, act_ref, pg_ref, bsend_ref, res_ref,
    acc_res, acc_back, sendsem, backsem, sem,
):
    wide_n, cap, width = send_ref.shape
    units = win_ref.shape[1]
    tile = 512
    w = lax.axis_index("wide")
    per = wide_n // chunks
    chunk_rows = per * cap
    loads = [
        pltpu.make_async_copy(a, b, sem.at[i])
        for i, (a, b) in enumerate(((cot_any, cot_ref), (win_any, win_ref), (wout_any, wout_ref)))
    ]
    for copy in loads:
        copy.start()
    enter(1, wide_n)

    def send_copy(k):
        return remote(
            send_ref.at[k], recv_ref.at[k], sendsem, k, "wide", flipped(w, k, wide_n)
        )

    def back_copy(k):
        return remote(
            bsend_ref.at[k], back_any.at[w], backsem, k, "wide", flipped(w, k, wide_n)
        )

    def send_step(i, carry):
        k = wide_n - 1 - i
        pick = expert_pick(flipped(w, k, wide_n), cap, slot_ref[...])
        send_ref[k] = dot(pick, routed_ref[...]).astype(bf16)
        send_copy(k).start()
        return carry

    lax.fori_loop(0, wide_n - 1, send_step, 0)
    pick = expert_pick(w, cap, slot_ref[...])
    recv_ref[0] = dot(pick, routed_ref[...]).astype(bf16)
    for copy in loads:
        copy.wait()
    lane = lax.broadcasted_iota(jnp.int32, (1, wr_ref.shape[1]), 1)
    hot = lane == w
    c0 = 0.7978845608028654
    c1 = c0 * 0.044715
    grouter_ref[...] = jnp.zeros_like(grouter_ref)

    def one_chunk(chunk, carry):
        first = chunk * per

        def arrive(j, inner):
            @pl.when(first + j > 0)
            def _():
                send_copy(first + j).wait_recv()

            return inner

        lax.fori_loop(0, per, arrive, 0)
        sources = pl.ds(first, per)
        here = pl.ds(pl.multiple_of(chunk * chunk_rows, chunk_rows), chunk_rows)
        x = recv_ref[sources].reshape(chunk_rows, width)
        cot = cot_ref[sources].reshape(chunk_rows, width).astype(f32)
        logits = jnp.where(lane < experts, dot(x, wr_ref[...]), -1e30)
        raised = jnp.exp(logits - jnp.max(logits, axis=-1, keepdims=True))
        probs = raised * (1.0 / jnp.sum(raised, axis=-1, keepdims=True))
        gate = jnp.sum(jnp.where(hot, probs, 0.0), axis=-1, keepdims=True)
        push_ref[here, :] = (gate * cot).astype(bf16)
        acc_res[...] = jnp.zeros_like(acc_res)
        acc_back[...] = jnp.zeros_like(acc_back)

        def hidden_tile(t, inner):
            cols = pl.ds(pl.multiple_of(t * tile, tile), tile)
            pre = dot(recv_ref[sources].reshape(chunk_rows, width), win_ref[:, cols])
            ag = dot(push_ref[here, :], wout_ref[cols, :], NT)
            sq = pre * pre
            th = jnp.tanh(pre * (c0 + c1 * sq))
            half = 0.5 + 0.5 * th
            act = (pre * half).astype(bf16)
            slope = half + pre * (0.5 - 0.5 * th * th) * (c0 + 3.0 * c1 * sq)
            pg = (ag * slope).astype(bf16)
            act_ref[here, cols] = act
            pg_ref[here, cols] = pg
            acc_res[...] += dot(act, wout_ref[cols, :])
            acc_back[...] += dot(pg, win_ref[:, cols], NT)
            return inner

        lax.fori_loop(0, units // tile, hidden_tile, 0)
        result = acc_res[...].astype(bf16).astype(f32)
        res_ref[sources] = (gate * result).astype(bf16).reshape(per, cap, width)
        gate_grad = jnp.sum(cot * result, axis=-1, keepdims=True)
        logit_grad = probs * (jnp.where(hot, gate_grad, 0.0) - gate * gate_grad)
        logit_grad = logit_grad.astype(bf16)
        back = acc_back[...].astype(bf16).astype(f32) + dot(logit_grad, wr_ref[...], NT)
        bsend_ref[sources] = back.astype(bf16).reshape(per, cap, width)
        grouter_ref[...] += dot(x, logit_grad, TN)

        def give(j, inner):
            @pl.when(first + j > 0)
            def _():
                back_copy(first + j).start()

            return inner

        lax.fori_loop(0, per, give, 0)
        return carry

    lax.fori_loop(0, chunks, one_chunk, 0)
    own = pltpu.make_async_copy(bsend_ref.at[0], back_any.at[w], sem.at[0])
    own.start()
    res_copy = pltpu.make_async_copy(res_ref, res_any, sem.at[1])
    res_copy.start()

    def weight_tile(t, carry):
        cols = pl.ds(pl.multiple_of(t * tile, tile), tile)
        win_ref[:, cols] = dot(
            recv_ref[...].reshape(wide_n * cap, width), pg_ref[:, cols], TN
        ).astype(bf16)
        wout_ref[cols, :] = dot(act_ref[:, cols], push_ref[...], TN).astype(bf16)
        return carry

    lax.fori_loop(0, units // tile, weight_tile, 0)
    gin_copy = pltpu.make_async_copy(win_ref, gin_any, sem.at[2])
    gin_copy.start()
    gout_copy = pltpu.make_async_copy(wout_ref, gout_any, sem.at[3])
    gout_copy.start()

    def finish_step(k, carry):
        send_copy(k).wait_send()
        back_copy(k).wait()
        return carry

    lax.fori_loop(1, wide_n, finish_step, 0)
    own.wait()
    res_copy.wait()
    gin_copy.wait()
    gout_copy.wait()


def run_experts(routed, slot_row, wr, cot_rows, win, wout, experts):
    wide_n, cap, width = cot_rows.shape
    units = win.shape[1]
    chunks = 4
    slots = wide_n * cap
    block = (wide_n, cap, width)
    step = slots // chunks
    return pl.pallas_call(
        functools.partial(expert_kernel, experts, chunks),
        in_specs=[vmem()] * 3 + [hbm()] * 3,
        out_specs=[hbm()] * 4 + [vmem()],
        out_shape=[
            jax.ShapeDtypeStruct(block, bf16),
            jax.ShapeDtypeStruct(block, bf16),
            jax.ShapeDtypeStruct((width, units), bf16),
            jax.ShapeDtypeStruct((units, width), bf16),
            jax.ShapeDtypeStruct((width, wr.shape[1]), f32),
        ],
        scratch_shapes=[
            pltpu.VMEM(block, bf16),
            pltpu.VMEM(block, bf16),
            pltpu.VMEM(block, bf16),
            pltpu.VMEM((slots, width), bf16),
            pltpu.VMEM((width, units), bf16),
            pltpu.VMEM((units, width), bf16),
            pltpu.VMEM((slots, units), bf16),
            pltpu.VMEM((slots, units), bf16),
            pltpu.VMEM(block, bf16),
            pltpu.VMEM(block, bf16),
            pltpu.VMEM((step, width), f32),
            pltpu.VMEM((step, width), f32),
            pltpu.SemaphoreType.DMA((2, wide_n)),
            pltpu.SemaphoreType.DMA((2, wide_n)),
            pltpu.SemaphoreType.DMA((4,)),
        ],
        compiler_params=params(collective_id=2, has_side_effects=True),
        name="experts",
    )(routed, slot_row, wr, cot_rows, win, wout)


def hidden_back_kernel(
    back_ref, slot_ref, hid_ref, cot_ref, att_ref, wo_ref, gain_ref,
    hg_ref, ag_ref, gwo_ref, ggain_ref, branch_ref,
):
    tokens, width = hid_ref.shape
    slots = back_ref.shape[0]
    step = 256
    gain = gain_ref[...]
    ggain_ref[...] = jnp.zeros_like(ggain_ref)

    def pull(i, carry):
        rows = pl.ds(pl.multiple_of(i * step, step), step)
        ids = lax.broadcasted_iota(jnp.int32, (step, slots), 1)
        pick = (ids == slot_ref[rows, :]).astype(f32).astype(bf16)
        upstream = dot(pick, back_ref[...])
        hidden = hid_ref[rows, :]
        inv = inverse_rms(hidden)
        scaled = upstream * gain
        inner = jnp.mean(scaled * hidden, axis=-1, keepdims=True)
        grad = cot_ref[rows, :].astype(f32) + inv * scaled - hidden * (inv * inv * inv * inner)
        ggain_ref[...] += jnp.sum(upstream * hidden * inv, axis=0, keepdims=True)
        hg_ref[rows, :] = grad
        low = grad.astype(bf16)
        branch_ref[rows, :] = low
        ag_ref[rows, :] = dot(low, wo_ref[...], NT).astype(bf16)
        return carry

    lax.fori_loop(0, tokens // step, pull, 0)

    def weight(i, carry):
        cols = pl.ds(pl.multiple_of(i * 256, 256), 256)
        gwo_ref[:, cols] = dot(att_ref[...], branch_ref[:, cols], TN).astype(bf16)
        return carry

    lax.fori_loop(0, width // 256, weight, 0)


def hidden_back(back, slot_col, hid, cot, att, wo, gain):
    tokens, width = hid.shape
    return pl.pallas_call(
        hidden_back_kernel,
        in_specs=[vmem()] * 7,
        out_specs=[vmem()] * 4,
        out_shape=[
            jax.ShapeDtypeStruct((tokens, width), f32),
            jax.ShapeDtypeStruct((tokens, width), bf16),
            jax.ShapeDtypeStruct((width, width), bf16),
            jax.ShapeDtypeStruct((1, width), f32),
        ],
        scratch_shapes=[pltpu.VMEM((tokens, width), bf16)],
        compiler_params=params(),
        name="hidden_back",
    )(back, slot_col, hid, cot, att, wo, gain)


def attention_backward_kernel(
    ag_ref, att_ref, p_ref, invl_ref, q_ref, k_ref, v_ref, tok_ref, gain_ref,
    wq_ref, wk_ref, wv_ref, gq_ref, gk_ref, gv_ref, part_ref, ggain_ref, diag_ref,
    dq_ref, dk_ref, dv_ref, strip_ref, normed_ref, kmask_ref, vext_ref, ds_ref,
):
    pair = pl.program_id(0)
    parts, seqs, span, width = tok_ref.shape
    total = parts * span
    table = diag_ref.shape[-1]
    low, masks = half_masks(128)
    lane = lax.broadcasted_iota(jnp.int32, (1, 128), 1)
    lanes = pl.ds(pl.multiple_of(pair * 128, 128), 128)
    strip_ref[...] = jnp.zeros_like(strip_ref)

    def one_sequence(s, carry):
        kp = k_ref[:, s, :, lanes].reshape(total, 128)
        vp = v_ref[:, s, :, lanes].reshape(total, 128)
        for hh in range(2):
            ones = (lane // 2 == 32 - 32 * hh).astype(f32)
            kmask_ref[hh * total : (hh + 1) * total, :] = kp * masks[hh]
            vext_ref[hh] = jnp.where(ones > 0, ones, vp.astype(f32)).astype(bf16)
        dk = [0.0, 0.0]
        dv = [0.0, 0.0]
        for block in range(parts // 2):
            rows = slice(block * 2 * span, (block + 1) * 2 * span)
            both = slice(2 * block, 2 * block + 2)
            qp = q_ref[both, s, :, lanes].reshape(2 * span, 128)
            inv = invl_ref[both, s, :, lanes].reshape(2 * span, 128)
            gp = ag_ref[both, s, :, lanes].reshape(2 * span, 128).astype(f32)
            gp = (gp * inv).astype(bf16)
            gf = gp.astype(f32)
            agree = gf * att_ref[both, s, :, lanes].reshape(2 * span, 128).astype(f32)
            for hh in range(2):
                delta = -jnp.sum(
                    jnp.where(low if hh == 0 else ~low, agree, 0.0), axis=-1, keepdims=True
                )
                high = delta.astype(bf16).astype(f32)
                ext = jnp.where(lane == 64 - 64 * hh, high, 0.0)
                ext = jnp.where(lane == 65 - 64 * hh, delta - high, ext)
                ext = jnp.where(low if hh == 0 else ~low, gf, ext).astype(bf16)
                raised = p_ref[0, s, rows, hh * total : (hh + 1) * total]
                score_grad = raised.astype(f32) * dot(ext, vext_ref[hh], NT)
                for r in range(2):
                    at = (parts - 1 - (2 * block + r)) * span
                    strip_ref[hh, :, at : at + total] += score_grad[r * span : (r + 1) * span]
                score_grad = score_grad.astype(bf16)
                ds_ref[:, hh * total : (hh + 1) * total] = score_grad
                dk[hh] = dk[hh] + dot(score_grad, qp, TN)
                dv[hh] = dv[hh] + dot(raised, gp, TN)
            dq = dot(ds_ref[...], kmask_ref[...])
            at_rows = pl.ds(pl.multiple_of(s * total + block * 2 * span, 2 * span), 2 * span)
            dq_ref[at_rows, lanes] = dq.astype(bf16)
        rows_all = pl.ds(pl.multiple_of(s * total, total), total)
        dk_ref[rows_all, lanes] = (jnp.where(low, dk[0], dk[1]) * (1.0 / LOG2E)).astype(bf16)
        dv_ref[rows_all, lanes] = jnp.where(low, dv[0], dv[1]).astype(bf16)
        return carry

    lax.fori_loop(0, seqs, one_sequence, 0)
    back = lax.broadcasted_iota(jnp.int32, (span, span), 0)
    flip = (back + lax.broadcasted_iota(jnp.int32, (span, span), 1) == span - 1).astype(f32)
    for hh in range(2):
        turned = lax.dot_general(
            flip, strip_ref[hh], NN, precision=lax.Precision.HIGHEST, preferred_element_type=f32
        )
        turned = pltpu.roll(turned, 0, 1, stride=1, stride_axis=0)
        diag_ref[0, hh : hh + 1, :] = jnp.sum(turned, axis=0, keepdims=True)

    @pl.when(pair == pl.num_programs(0) - 1)
    def _():
        gain = gain_ref[...]
        ggain_ref[...] = jnp.zeros_like(ggain_ref)

        def pull(step, carry):
            s, n = step // (parts // 2), step % (parts // 2)
            x = tok_ref[pl.ds(2 * n, 2), s].reshape(2 * span, width).astype(f32)
            inv = inverse_rms(x)
            rows = pl.ds(pl.multiple_of(step * 2 * span, 2 * span), 2 * span)
            normed_ref[rows, :] = (x * inv * gain).astype(bf16)
            upstream = dot(dq_ref[rows, :], wq_ref[...], NT)
            upstream += dot(dk_ref[rows, :], wk_ref[...], NT)
            upstream += dot(dv_ref[rows, :], wv_ref[...], NT)
            scaled = upstream * gain
            inner = jnp.mean(scaled * x, axis=-1, keepdims=True)
            grad = inv * scaled - x * (inv * inv * inv * inner)
            ggain_ref[...] += jnp.sum(upstream * x * inv, axis=0, keepdims=True)
            grad = grad.astype(bf16).reshape(2, span, width)
            part_ref[pl.ds(2 * n, 2), s] = grad
            return carry

        lax.fori_loop(0, seqs * (parts // 2), pull, 0)

        def weight(i, carry):
            cols = pl.ds(pl.multiple_of(i * 256, 256), 256)
            gq_ref[:, cols] = dot(normed_ref[...], dq_ref[:, cols], TN).astype(bf16)
            gk_ref[:, cols] = dot(normed_ref[...], dk_ref[:, cols], TN).astype(bf16)
            gv_ref[:, cols] = dot(normed_ref[...], dv_ref[:, cols], TN).astype(bf16)
            return carry

        lax.fori_loop(0, width // 256, weight, 0)


def attention_backward(ag, att, p, invl, q, k, v, tok, gain, wq, wk, wv, table):
    parts, seqs, span, width = tok.shape
    total = parts * span
    pairs = p.shape[0]
    square = jax.ShapeDtypeStruct((width, width), bf16)
    rows = pltpu.VMEM((seqs * total, width), bf16)
    return pl.pallas_call(
        attention_backward_kernel,
        grid=(pairs,),
        in_specs=[
            vmem(),
            vmem(),
            pl.BlockSpec((1, seqs, total, 2 * total), lambda i: (i, 0, 0, 0)),
        ]
        + [vmem()] * 9,
        out_specs=[vmem()] * 5 + [pl.BlockSpec((1, 2, table), lambda i: (i, 0, 0))],
        out_shape=[
            square, square, square,
            jax.ShapeDtypeStruct((parts, seqs, span, width), bf16),
            jax.ShapeDtypeStruct((1, width), f32),
            jax.ShapeDtypeStruct((pairs, 2, table), f32),
        ],
        scratch_shapes=[
            rows, rows, rows, pltpu.VMEM((2, span, table), f32), rows,
            pltpu.VMEM((2 * total, 128), bf16),
            pltpu.VMEM((2, total, 128), bf16),
            pltpu.VMEM((2 * span, 2 * total), bf16),
        ],
        compiler_params=params(),
        name="attention_backward",
    )(ag, att, p, invl, q, k, v, tok, gain, wq, wk, wv)


def finish_kernel(res_ref, slot_ref, hid_ref, out_ref):
    tokens, width = hid_ref.shape
    slots = res_ref.shape[0]
    step = 256

    def add(i, carry):
        rows = pl.ds(pl.multiple_of(i * step, step), step)
        ids = lax.broadcasted_iota(jnp.int32, (step, slots), 1)
        pick = (ids == slot_ref[rows, :]).astype(f32).astype(bf16)
        out_ref[rows, :] = hid_ref[rows, :] + dot(pick, res_ref[...])
        return carry

    lax.fori_loop(0, tokens // step, add, 0)


def finish(res, slot_col, hid):
    return pl.pallas_call(
        finish_kernel,
        in_specs=[vmem()] * 3,
        out_specs=vmem(),
        out_shape=jax.ShapeDtypeStruct(hid.shape, f32),
        compiler_params=params(),
        name="finish",
    )(res, slot_col, hid)


def body(
    tokens, lengths, routes, bucket_table, attn_gain, query_weight, key_weight, value_weight,
    output_weight, relative_bias, expert_gain, router_weight, experts_in, experts_out, cotangent,
):
    seq_count, span, width = tokens.shape
    narrow_n = lax.axis_size("narrow")
    wide_n = lax.axis_size("wide")
    seqs = seq_count // narrow_n
    heads = relative_bias.shape[1]
    buckets = relative_bias.shape[0]
    experts = router_weight.shape[1]
    tok_count = seq_count * span
    capacity = 5 * tok_count // (4 * experts)
    cap = -(-capacity // 16) * 16
    slots = experts * cap
    table = 2 * span * narrow_n
    gain_a = attn_gain.astype(f32).reshape(1, width)
    gain_e = expert_gain.astype(f32).reshape(1, width)
    router = jnp.pad(router_weight, ((0, 0), (0, -experts % 128)))

    def swap(array):
        return lax.all_to_all(array, "narrow", split_axis=0, concat_axis=0, tiled=True)

    def trade(array):
        array = array.reshape(wide_n, -1, width)
        return lax.all_to_all(array, "wide", split_axis=0, concat_axis=0, tiled=True).reshape(
            -1, width
        )

    table_ids = jnp.pad(bucket_table, (0, 1))
    offset_hot = (table_ids[None, :] == jnp.arange(buckets, dtype=jnp.int32)[:, None]).astype(bf16)
    diag = dot(relative_bias, offset_hot, TN).reshape(heads // 2, 2, table)
    route_ids = routes.reshape(tok_count)
    onehot = route_ids[:, None] == jnp.arange(experts, dtype=jnp.int32)[None, :]
    counts = jnp.cumsum(onehot.astype(jnp.int32), axis=0)
    position = jnp.sum(jnp.where(onehot, counts - 1, 0), axis=-1)
    slot = jnp.where(position < capacity, route_ids * cap + position, slots)
    slot_row, slot_col = slot.reshape(1, tok_count), slot.reshape(tok_count, 1)

    flat_cot = cotangent.reshape(tok_count, width)
    tok_quad = tokens.reshape(narrow_n, seqs, span, width)
    tok_seq, att_seq, att_pos, hidden, routed, cot_rows, q, k, v, invl, probs = forward(
        lengths, tok_quad, flat_cot, slot_row, diag * LOG2E, gain_a, gain_e,
        query_weight, key_weight, value_weight, output_weight, wide_n, cap,
    )
    attended = att_pos.reshape(tok_count, width)
    res, back_rows, term_in, term_out, router_grad = run_experts(
        routed, slot_row, router, cot_rows, experts_in[0], experts_out[0], experts
    )
    back_rows = back_rows.reshape(slots, width)
    me = lax.axis_index("wide")
    order = jnp.arange(wide_n, dtype=jnp.int32) ^ me
    res_rows = trade(res[order])
    hidden_grad, att_grad, output_grad, gain_second = hidden_back(
        back_rows, slot_col, hidden, flat_cot, attended, output_weight, gain_e
    )
    layer_output = finish(res_rows, slot_col, hidden).reshape(seq_count, span, width)
    ag_seq = swap(att_grad.reshape(seq_count, span, width)).reshape(narrow_n, seqs, span, width)
    grad_query, grad_key, grad_value, part, gain_first, diag_grad = attention_backward(
        ag_seq, att_seq, probs, invl, q, k, v, tok_seq, gain_a, query_weight, key_weight, value_weight, table
    )
    part = swap(part.reshape(seq_count, span, width))
    input_grad = hidden_grad.reshape(seq_count, span, width) + part.astype(f32)
    relative_grad = lax.dot_general(
        offset_hot.astype(f32),
        diag_grad.reshape(heads, table),
        NT,
        precision=lax.Precision.HIGHEST,
        preferred_element_type=f32,
    )

    def scatter(array, dim=0):
        return lax.psum_scatter(
            array.astype(bf16), "narrow", scatter_dimension=dim, tiled=True
        ).astype(f32)

    grad_experts_in = scatter(term_in)[None]
    grad_experts_out = scatter(term_out)[None]
    shares = tuple(
        scatter(item)
        for item in (
            grad_query, grad_key, grad_value, output_grad, router_grad[:, :experts],
            relative_grad, gain_first[0], gain_second[0],
        )
    )
    totals = lax.psum(shares, "wide")
    return (
        layer_output,
        input_grad,
        totals[6],
        totals[0],
        totals[1],
        totals[2],
        totals[3],
        totals[5],
        totals[7],
        totals[4],
        grad_experts_in,
        grad_experts_out,
    )


def solution(mesh):
    token = P("wide", "narrow", None)
    expert = P("wide", None, None)
    row, vector = P("narrow", None), P("narrow")
    return jax.shard_map(
        body,
        mesh=mesh,
        in_specs=(token, P("wide"), token) + (P(),) * 9 + (expert, expert, token),
        out_specs=(
            token, token, vector, row, row, row, row, row, vector, row,
            P("wide", "narrow", None), P("wide", "narrow", None),
        ),
        check_vma=False,
    )
```

time: 605 us -> 473 us (0.78)
  waiting for transfers between devices: 157 us -> 45.4 us
  blocking collectives: 201 us -> 142 us
  Pallas kernels: 175 us -> 217 us
  starting transfers between devices: 26.9 us -> 19.4 us
    all_to_all x3 -> x1, waiting for transfers between devices: 122 us -> 22.7 us  [trade(): lax.all_to_all(array, 'wide', split_axis=0, concat_axis=0, tiled=True)]
    all_to_all x1 -> x0, blocking collectives: 49.1 us -> none  [trade(): lax.all_to_all(array, 'wide', split_axis=0, concat_axis=0, tiled=True)]
    pallas_call x3 -> x2, Pallas kernels: 104 us -> 148 us  [the longest x1 92.6 us: run_experts(): pl.pallas_call(functools.partial(expert_kernel, experts, chunks), in_spec...]
    all_to_all x3 -> x1, waiting for transfers between devices: 32.2 us -> 20.3 us  [swap(): lax.all_to_all(array, 'narrow', split_axis=0, concat_axis=0, tiled=True)]
    all_to_all x3 -> x1, starting transfers between devices: 11.8 us -> 3.71 us  [swap(): lax.all_to_all(array, 'narrow', split_axis=0, concat_axis=0, tiled=True)]
    unnamed x1, blocking collectives: 19.3 us -> 12 us
    all_to_all x3 -> x1, starting transfers between devices: 14.7 us -> 15.4 us  [trade(): lax.all_to_all(array, 'wide', split_axis=0, concat_axis=0, tiled=True)]
  transfers between devices with their start and end apart: 13 -> 9, of which waited for: 5 -> 2; matrix products, arithmetic and copies ran while one was open for 3% -> 3% of each run, Pallas kernels for 13% -> 15%
where the time goes in v2:
time: 473 us; the launch traced here: 472 us
  Pallas kernels  217 us (46%)
  blocking collectives  142 us (30%)
  waiting for transfers between devices  45.4 us (10%)
  starting transfers between devices  19.4 us (4%)
  other arithmetic  17.9 us (4%)
  between operations  15.6 us (3%)
  local copies, waits for them, and re-layouts  13.9 us (3%)
    psum x1, blocking collectives, body(): totals = lax.psum(shares, 'wide')  103 us
    pallas_call x1, Pallas kernels, run_experts(): pl.pallas_call(functools.partial(expert_kernel, experts, chunks), in_spec...  92.6 us
    pallas_call x1, Pallas kernels, forward(): pl.pallas_call(functools.partial(forward_kernel, wide_n), in_specs=[pl.Bl...  55.4 us
    pallas_call x1, Pallas kernels, attention_backward(): pl.pallas_call(attention_backward_kernel, grid=(pairs,), in_specs=[vmem()...  47.7 us
    all_to_all x1, blocking collectives, swap(): lax.all_to_all(array, 'narrow', split_axis=0, concat_axis=0, tiled=True)  26.6 us
    all_to_all x1, waiting for transfers between devices, trade(): lax.all_to_all(array, 'wide', split_axis=0, concat_axis=0, tiled=True)  22.7 us
    all_to_all x1, waiting for transfers between devices, swap(): lax.all_to_all(array, 'narrow', split_axis=0, concat_axis=0, tiled=True)  20.3 us
    all_to_all x1, starting transfers between devices, trade(): lax.all_to_all(array, 'wide', split_axis=0, concat_axis=0, tiled=True)  15.4 us
  transfers between devices with their start and end apart: 9, of which 2 were waited for; matrix products, arithmetic and copies ran while one was open for 3% of the time, Pallas kernels for 15%

profile of v2, /device:TPU:0, one launch (start us, length us, event | category | flops | bytes accessed | tf_op | source)
XLA Modules:
  0.0 472.4 jit_solution(2945469307634597958)
XLA Ops:
  7.2 1.3 reshape.178.gain_a_ref.gain_ref
  8.5 1.3 reshape.180.gain_e_ref.gain_ref
  11.8 2.3 reduce-window.6
  15.4 0.9 copy.36
  18.3 55.4 %forward.1 = (bf16[4,2,128,768]{3,2,1,0:T(8,128)(2,1)}, bf16[4,2,128,768]{3,2,1,0:T(8,128)(2,1)}, bf16[4,2,128,768]{3,2,1,0:T(8,128)(2,1)}, f32[1024,768]{1,0:T(...) custom-call(s32[8]{0:T(128)} %lens_ref.1, ...), custom_call_target="tpu_custom_call" | custom-call | tf_op jit(solution)/shard_map/forward/pallas_call | solution.py:267
  73.7 92.6 %experts.1 = (bf16[8,160,768]{2,1,0:T(8,128)(2,1)}, bf16[8,160,768]{2,1,0:T(8,128)(2,1)}, bf16[768,3072]{1,0:T(8,128)(2,1)}, bf16[3072,768]{1,0:T(8,128)(2,1)}, f32[768,128]{1,0:T(8,128)}) custom-call(bf16[1024,768]{1,0:T(8,128)(2,1)} %get-tuple-element.38.routed_ref, s32[1,1024]{1,0:T(1,128)} %compare_select_fusion.slot_ref, bf16[768,128]{1,0:T(8,128)(2,1)} %pad.9.wr_ref, ...), custom_call_target="tpu_custom_call" | custom-call | tf_op jit(solution)/shard_map/experts/pallas_call | solution.py:445
  166.4 1.7 slice.19
  169.5 14.1 %hidden_back.1 = (f32[1024,768]{1,0:T(8,128)}, bf16[1024,768]{1,0:T(8,128)(2,1)}, bf16[768,768]{1,0:T(8,128)(2,1)}, f32[1,768]{1,0:T(1,128)}) custom-call(bf16[1280,768]{1,0:T(8,128)(2,1)} %bitcast.55, s32[1024,1]{1,0:T(8,128)} %add_select_fusion.slot_ref, f32[1024,768]{1,0:T(8,128)} %get-tuple-element.41.hid_ref, bf16[1024,768]{1,0:T(8,128)(2,1)} %bitcast.50, ...), custom_call_target="tpu_custom_call" | custom-call | tf_op jit(solution)/shard_map/hidden_back/pallas_call | solution.py:517
  183.6 26.6 %all_to_all.15 = bf16[8,128,768]{2,1,0:T(8,128)(2,1)} all-to-all(bf16[8,128,768]{2,1,0:T(8,128)(2,1)} %bitcast.57), channel_id=1, replica_groups=mesh['wide'=8,'narrow'=4] {'narrow'}, dimensions={0} | all-to-all | bytes 3145728 | tf_op jit(solution)/shard_map/all_to_all | solution.py:714
  210.3 47.7 %attention_backward.1 = (bf16[768,768]{1,0:T(8,128)(2,1)}, bf16[768,768]{1,0:T(8,128)(2,1)}, bf16[768,768]{1,0:T(8,128)(2,1)}, bf16[4,2,128,768]{3,2,1,0:T(8,128...) custom-call(bf16[4,2,128,768]{3,2,1,0:T(8,128)(2,1)} %bitcast.48, bf16[4,2,128,768]{3,2,1,0:T(8,128)(2,1)} %get-tuple-element.46.att_ref, ...), custom_call_target="tpu_custom_call" | custom-call | tf_op jit(solution)/shard_map/attention_backward/pallas_call | solution.py:640
  260.5 3.7 all-to-all-start.2
  264.3 1.9 gather_fusion
  266.2 20.3 %all-to-all-done.2 = bf16[8,128,768]{2,1,0:T(8,128)(2,1)S(1)} async-done(((bf16[8,128,768]{2,1,0:T(8,128)(2,1)}), bf16[8,128,768]{2,1,0:T(8,128)(2,1)S(1)}, u32[]{:S(2)}, u32[]{:S(2)}) %all-to-all-start.2) | async-done | bytes 1572896 | tf_op jit(solution)/shard_map/all_to_all | solution.py:714
  286.5 15.4 %all-to-all-start = ((bf16[8,160,768]{2,1,0:T(8,128)(2,1)}), bf16[8,160,768]{2,1,0:T(8,128)(2,1)S(1)}, u32[]{:S(2)}, u32[]{:S(2)}) async-start(bf16[8,160,768]{2,1,0:T(8,128)(2,1)} %gather_fusion), calls=%async_computation | async-start | bytes 3932160 | tf_op jit(solution)/shard_map/all_to_all | solution.py:718
  303.9 1.5 reshape.176
  306.0 1.0 convolution_convert_fusion
  307.0 12.0 %all-reduce.6 = (bf16[768]{0:T(1024)(128)(2,1)}, bf16[32,12]{1,0:T(8,128)(2,1)}, bf16[768]{0:T(1024)(128)(2,1)}) all-reduce(bf16[768]{0:T(1024)(128)(2,1)} %convert_reduce_fusion.1, bf16[32,12]{1,0:T(8,128)(2,1)S(1)} %convolution_convert_fusion, ...), channel_id=2, replica_groups=mesh['wide'=8,'narrow'=4] {'narrow'}, use_global_device_ids=true, to_apply=%region_3.4.clone | all-reduce | flops 1920 | bytes 7680
  320.5 4.0 convert_add_fusion
  324.4 22.7 %all-to-all-done = bf16[8,160,768]{2,1,0:T(8,128)(2,1)S(1)} async-done(((bf16[8,160,768]{2,1,0:T(8,128)(2,1)}), bf16[8,160,768]{2,1,0:T(8,128)(2,1)S(1)}, u32[]{:S(2)}, u32[]{:S(2)}) %all-to-all-start) | async-done | bytes 1966112 | tf_op jit(solution)/shard_map/all_to_all | solution.py:718
  347.2 1.3 copy-done.2
  348.5 7.5 %finish.1 = f32[1024,768]{1,0:T(8,128)} custom-call(bf16[1280,768]{1,0:T(8,128)(2,1)} %bitcast.47, s32[1024,1]{1,0:T(8,128)} %add_select_fusion.slot_ref, f32[1024,768]{1,0:T(8,128)} %get-tuple-element.41.hid_ref), custom_call_target="tpu_custom_call" | custom-call | tf_op jit(solution)/shard_map/finish/pallas_call | solution.py:683
  356.0 103.1 %all-reduce.8 = (f32[192]{0:T(256)}, f32[192,768]{1,0:T(8,128)}, f32[192,768]{1,0:T(8,128)}, f32[192,768]{1,0:T(8,128)}, f32[192,768]{1,0:T(8,128)}, /*index=5*/...) all-reduce(f32[192]{0:T(256)S(1)} %get-tuple-element.112, ...), channel_id=1, replica_groups=mesh['wide'=8,'narrow'=4] {'wide'}, use_global_device_ids=true, to_apply=%region_4.5 | all-reduce | flops 591840 | bytes 3552000 | tf_op jit(solution)/shard_map/psum | solution.py:778
  459.8 2.9 bitcast_convert_fusion
  462.6 2.9 bitcast_convert_fusion.1
  (60 shorter events, 12.7 us)
Async XLA Ops:
  7.2 7.4 %copy-start = (bf16[32,12]{0,1:T(8,128)(2,1)S(1)}, bf16[32,12]{0,1:T(8,128)(2,1)}, u32[]{:S(2)}) copy-start(bf16[32,12]{0,1:T(8,128)(2,1)} %param.24) | copy-start | bytes 2308
  7.2 296.7 %reduce-scatter.16.cloned.1.call-start = ((), (), s32[]{:S(2)}) async-start(), calls=%async_computation.14 | async-start | bytes 245760 | tf_op jit(solution)/shard_map/reduce_scatter | solution.py:765
  168.1 152.4 %reduce-scatter.14.cloned.1.call-start = ((), (), s32[]{:S(2)}) async-start(), calls=%async_computation.13 | async-start | bytes 1474560 | tf_op jit(solution)/shard_map/reduce_scatter | solution.py:765
  183.6 172.4 %reduce-scatter.8.cloned.1.call-start = ((), (), s32[]{:S(2)}) async-start(), calls=%async_computation.10 | async-start | bytes 1474560 | tf_op jit(solution)/shard_map/reduce_scatter | solution.py:765
  258.0 98.0 %reduce-scatter.10.cloned.1.call-start = ((), (), s32[]{:S(2)}) async-start(), calls=%async_computation.11 | async-start | bytes 1474560 | tf_op jit(solution)/shard_map/reduce_scatter | solution.py:765
  258.6 97.4 %reduce-scatter.12.cloned.1.call-start = ((), (), s32[]{:S(2)}) async-start(), calls=%async_computation.12 | async-start | bytes 1474560 | tf_op jit(solution)/shard_map/reduce_scatter | solution.py:765
  259.2 200.6 %reduce-scatter.20.cloned.1.call-start = ((), (), s32[]{:S(2)}) async-start(), calls=%async_computation.16 | async-start | bytes 5898240 | tf_op jit(solution)/shard_map/reduce_scatter | solution.py:765
  259.8 202.9 %reduce-scatter.18.cloned.1.call-start = ((), (), s32[]{:S(2)}) async-start(), calls=%async_computation.15 | async-start | bytes 5898240 | tf_op jit(solution)/shard_map/reduce_scatter | solution.py:765
  260.5 3.8 copy-start.3
  260.5 26.0 %all-to-all-start.2 = ((bf16[8,128,768]{2,1,0:T(8,128)(2,1)}), bf16[8,128,768]{2,1,0:T(8,128)(2,1)S(1)}, u32[]{:S(2)}, u32[]{:S(2)}) async-start(bf16[8,128,768]{2,1,0:T(8,128)(2,1)} %bitcast.56), calls=%async_computation.2 | async-start | bytes 3145728 | tf_op jit(solution)/shard_map/all_to_all | solution.py:714
  266.2 35.7 %copy-start.8 = (u32[32]{0:T(128)S(1)}, u32[32]{0:T(128)}, u32[]{:S(2)}) copy-start(u32[32]{0:T(128)} %constant.33) | copy-start | bytes 388
  266.2 37.6 %copy-start.6 = (f32[1,768]{1,0:T(1,128)S(1)}, f32[1,768]{1,0:T(1,128)}, u32[]{:S(2)}) copy-start(f32[1,768]{1,0:T(1,128)} %get-tuple-element.60) | copy-start | bytes 9220
  266.2 39.2 %copy-start.7 = (f32[1,768]{1,0:T(1,128)S(1)}, f32[1,768]{1,0:T(1,128)}, u32[]{:S(2)}) copy-start(f32[1,768]{1,0:T(1,128)} %get-tuple-element.54) | copy-start | bytes 9220
  286.5 60.7 %all-to-all-start = ((bf16[8,160,768]{2,1,0:T(8,128)(2,1)}), bf16[8,160,768]{2,1,0:T(8,128)(2,1)S(1)}, u32[]{:S(2)}, u32[]{:S(2)}) async-start(bf16[8,160,768]{2,1,0:T(8,128)(2,1)} %gather_fusion), calls=%async_computation | async-start | bytes 3932160 | tf_op jit(solution)/shard_map/all_to_all | solution.py:718
  347.2 1.3 copy-start.2
  348.5 7.6 %copy-start.4 = (bf16[192,768]{1,0:T(8,128)(2,1)S(1)}, bf16[192,768]{1,0:T(8,128)(2,1)}, u32[]{:S(2)}) copy-start(bf16[192,768]{1,0:T(8,128)(2,1)} %reduce-scatter.14.cloned.1.call-done) | copy-start | bytes 884740
  348.5 7.6 %copy-start.5 = (bf16[192,8]{1,0:T(8,128)(2,1)S(1)}, bf16[192,8]{1,0:T(8,128)(2,1)}, u32[]{:S(2)}) copy-start(bf16[192,8]{1,0:T(8,128)(2,1)} %reduce-scatter.16.cloned.1.call-done) | copy-start | bytes 9220
  459.8 5.8 %copy-start.1 = (bf16[32,12]{0,1:T(8,128)(2,1)S(1)}, bf16[32,12]{0,1:T(8,128)(2,1)}, u32[]{:S(2)}) copy-start(bf16[32,12]{0,1:T(8,128)(2,1)} %param.24) | copy-start | bytes 2308
Sparse Core Ops, SparseCore 0:
  168.2 29.9 reduce-scatter.15
  201.3 25.7 reduce-scatter.13
  258.1 33.4 reduce-scatter.7
  294.0 29.4 reduce-scatter.9
  326.1 25.7 reduce-scatter.11
  354.2 47.8 reduce-scatter.19
  404.8 47.8 reduce-scatter.17

commit v3 on v2

--- a/solution.py
+++ b/solution.py
@@ -204,7 +204,7 @@
                     pbuf[s, rows, hh * total : (hh + 1) * total] = raised.astype(bf16)
                 mixed = dot(pbuf[s, rows, :], vext[...])
                 inv = 1.0 / mixed[:, 128:]
-                invl_ref[both, s, :, lanes] = inv.reshape(2, span, 128)
+                invl_ref[both, s, :, lanes] = inv.astype(bf16).reshape(2, span, 128)
                 attseq[both, s, :, lanes] = (mixed[:, :128] * inv).astype(bf16).reshape(2, span, 128)
             pltpu.make_async_copy(pbuf.at[s], p_any.at[pair, s], psem.at[s]).start()
             return inner
@@ -261,7 +261,7 @@
     quad = (parts, seqs, span, width)
     shapes = [
         (quad, bf16), (quad, bf16), (quad, bf16), ((tokens, width), f32), ((tokens, width), bf16),
-        ((wide_n, cap, width), bf16), (quad, bf16), (quad, bf16), (quad, bf16), (quad, f32),
+        ((wide_n, cap, width), bf16), (quad, bf16), (quad, bf16), (quad, bf16), (quad, bf16),
         ((pairs, seqs, total, 2 * total), bf16),
     ]
     return pl.pallas_call(
@@ -275,7 +275,7 @@
             pltpu.VMEM(quad, bf16),
             pltpu.VMEM(quad, bf16),
             pltpu.VMEM(quad, bf16),
-            pltpu.VMEM(quad, f32),
+            pltpu.VMEM(quad, bf16),
             pltpu.VMEM(quad, bf16),
             pltpu.VMEM(quad, bf16),
             pltpu.VMEM((tokens, width), f32),
@@ -475,219 +475,515 @@
     )(routed, slot_row, wr, cot_rows, win, wout)
 
 
-def hidden_back_kernel(
-    back_ref, slot_ref, hid_ref, cot_ref, att_ref, wo_ref, gain_ref,
-    hg_ref, ag_ref, gwo_ref, ggain_ref, branch_ref,
+def link(src, dst, send_sem, recv_sem, axis, peer):
+    return pltpu.make_async_remote_copy(
+        src_ref=src,
+        dst_ref=dst,
+        send_sem=send_sem,
+        recv_sem=recv_sem,
+        device_id={axis: peer},
+        device_id_type=MESH,
+    )
+
+
+def padded(v):
+    return -(-v // 16) * 16
+
+
+class Sums:
+    def __init__(self, wide_n, refs, sems):
+        self.terms, self.near, self.far, self.mine, self.given, self.whole = refs
+        self.near_sem, self.far_sem, self.piece_sem, self.gather_sem = sems
+        self.wide_n = wide_n
+        self.n, self.w = lax.axis_index("narrow"), lax.axis_index("wide")
+        self.core, self.half = self.n % 2, self.n // 2
+        _, _, self.blocks, self.rows, _ = self.terms.shape
+        self.piece = self.given.shape[2]
+
+    def near_copy(self, g, side):
+        return link(
+            self.terms.at[g, 2 * side + 1 - self.core], self.near.at[g, side],
+            self.near_sem.at[0, g, side], self.near_sem.at[1, g, side],
+            "narrow", flipped(self.n, 1, 4),
+        )
+
+    def far_copy(self, g):
+        return link(
+            self.terms.at[g, 2 * (1 - self.half) + self.core], self.far.at[g],
+            self.far_sem.at[0, g], self.far_sem.at[1, g], "narrow", flipped(self.n, 2, 4),
+        )
+
+    def piece_copy(self, g, k):
+        peer = flipped(self.w, k, self.wide_n)
+        at = pl.ds(pl.multiple_of(peer * self.piece, 16), self.piece)
+        return link(
+            self.mine.at[g, at], self.given.at[g, k],
+            self.piece_sem.at[0, g, k], self.piece_sem.at[1, g, k], "wide", peer,
+        )
+
+    def gather_copy(self, g, k):
+        at = pl.ds(pl.multiple_of(self.w * self.piece, 16), self.piece)
+        return link(
+            self.whole.at[g, at], self.whole.at[g, at],
+            self.gather_sem.at[0, g, k], self.gather_sem.at[1, g, k],
+            "wide", flipped(self.w, k, self.wide_n),
+        )
+
+    def each(self, f):
+        def step(k, carry):
+            f(k)
+            return carry
+
+        lax.fori_loop(1, self.wide_n, step, 0)
+
+    def start(self, g):
+        for side in (0, 1):
+            self.near_copy(g, side).start()
+
+    def to_far(self, g):
+        for side in (1 - self.half, self.half):
+            self.near_copy(g, side).wait()
+            at = 2 * side + self.core
+            total = self.terms[g, at].astype(f32) + self.near[g, side].astype(f32)
+            self.terms[g, at] = total.astype(bf16)
+            if side is not self.half:
+                self.far_copy(g).start()
+
+    def to_pieces(self, g):
+        self.far_copy(g).wait()
+        total = self.terms[g, 2 * self.half + self.core].astype(f32) + self.far[g].astype(f32)
+        rows = self.blocks * self.rows
+        self.mine[g, :rows] = total.astype(bf16).reshape(rows, 128)
+        self.each(lambda k: self.piece_copy(g, k).start())
+
+    def to_gather(self, g):
+        at = pl.ds(pl.multiple_of(self.w * self.piece, 16), self.piece)
+        self.each(lambda k: self.piece_copy(g, k).wait())
+
+        def add(k, total):
+            return total + self.given[g, k].astype(f32)
+
+        total = lax.fori_loop(1, self.wide_n, add, self.mine[g, at].astype(f32))
+        self.whole[g, at] = total.astype(bf16)
+        self.each(lambda k: self.gather_copy(g, k).start())
+
+    def finish(self, g):
+        self.each(lambda k: self.gather_copy(g, k).wait())
+
+    @staticmethod
+    def scratch(groups, blocks, rows, wide_n):
+        piece = padded(-(-blocks * rows // wide_n))
+        return [
+            pltpu.VMEM((groups, 4, blocks, rows, 128), bf16),
+            pltpu.VMEM((groups, 2, blocks, rows, 128), bf16),
+            pltpu.VMEM((groups, blocks, rows, 128), bf16),
+            pltpu.VMEM((groups, wide_n * piece, 128), bf16),
+            pltpu.VMEM((groups, wide_n, piece, 128), bf16),
+            pltpu.VMEM((groups, wide_n * piece, 128), bf16),
+        ], [
+            pltpu.SemaphoreType.DMA((2, groups, 2)),
+            pltpu.SemaphoreType.DMA((2, groups)),
+            pltpu.SemaphoreType.DMA((2, groups, wide_n)),
+            pltpu.SemaphoreType.DMA((2, groups, wide_n)),
+        ]
+
+
+def backward_kernel(
+    wide_n, back_any, slot_ref, hid_any, cot_any, att_any, attseq_any, p_any, invl_any,
+    q_any, k_any, v_any, tok_any, res_any, wo_ref, wq_ref, wk_ref, wv_ref, gain_a_ref, gain_e_ref,
+    router_ref, hot_ref,
+    out_any, igrad_any, big_any, small_any, resland_any,
+    back_ref, hid_ref, cot_ref, att_ref, attseq_ref, invl_ref, q_ref, k_ref, v_ref, tok_ref,
+    agsend, agbuf, partbuf, turned_ref, dk_ref, dv_ref, pbuf, acc_ref, diag_ref,
+    kmask_ref, vext_ref, ds_ref, gains_ref, smallout, loadsem, psem, agsem, partsem,
+    ressem, *rest,
 ):
-    tokens, width = hid_ref.shape
-    slots = back_ref.shape[0]
-    step = 256
-    gain = gain_ref[...]
-    ggain_ref[...] = jnp.zeros_like(ggain_ref)
-
-    def pull(i, carry):
-        rows = pl.ds(pl.multiple_of(i * step, step), step)
-        ids = lax.broadcasted_iota(jnp.int32, (step, slots), 1)
+    parts, seqs, span, width = tok_ref.shape
+    total = parts * span
+    block_rows = seqs * span
+    pairs = width // 128
+    slots = back_ref.shape[0] * back_ref.shape[1]
+    rows_n = width // parts
+    n, w = lax.axis_index("narrow"), lax.axis_index("wide")
+    big = Sums(wide_n, rest[0:6], rest[12:16])
+    small = Sums(wide_n, rest[6:12], rest[16:20])
+    loads = [
+        pltpu.make_async_copy(a, b, loadsem.at[i])
+        for i, (a, b) in enumerate(
+            (
+                (back_any, back_ref), (hid_any, hid_ref), (cot_any, cot_ref), (att_any, att_ref),
+                (attseq_any, attseq_ref), (invl_any, invl_ref), (q_any, q_ref), (k_any, k_ref),
+                (v_any, v_ref), (tok_any, tok_ref),
+            )
+        )
+    ]
+    for copy in loads:
+        copy.start()
+
+    def block_of(phase):
+        return n // 2 + phase * (1 - 2 * (n // 2))
+
+    def p_copy(i):
+        at = pl.ds(pl.multiple_of(block_of(i // pairs) * 2 * span, 2 * span), 2 * span)
+        return pltpu.make_async_copy(p_any.at[i % pairs, :, at], pbuf.at[i % 2], psem.at[i % 2])
+
+    p_copy(0).start()
+    enter(parts, wide_n)
+
+    def res_copy(k):
+        return remote(
+            res_any.at[k], resland_any.at[w], ressem, k, "wide", flipped(w, k, wide_n)
+        )
+
+    def res_start(k, carry):
+        res_copy(k).start()
+        return carry
+
+    lax.fori_loop(1, wide_n, res_start, 0)
+    res_own = pltpu.make_async_copy(res_any.at[0], resland_any.at[w], loadsem.at[10])
+    res_own.start()
+
+    def ag_copy(k):
+        peer = flipped(n, k, parts)
+        return remote(agsend.at[peer], agbuf.at[n], agsem, k, "narrow", peer)
+
+    def rows_of(src):
+        return pl.ds(pl.multiple_of(src * block_rows, block_rows), block_rows)
+
+    def picked(rows):
+        ids = lax.broadcasted_iota(jnp.int32, (block_rows, slots), 1)
         pick = (ids == slot_ref[rows, :]).astype(f32).astype(bf16)
-        upstream = dot(pick, back_ref[...])
+        return dot(pick, back_ref[...].reshape(slots, width))
+
+    gain_a, gain_e = gain_a_ref[...], gain_e_ref[...]
+    gains_ref[...] = jnp.zeros_like(gains_ref)
+    for copy in loads[:3]:
+        copy.wait()
+    for k in range(parts - 1, -1, -1):
+        src = flipped(n, k, parts)
+        rows = rows_of(src)
+        upstream = picked(rows)
         hidden = hid_ref[rows, :]
         inv = inverse_rms(hidden)
-        scaled = upstream * gain
+        scaled = upstream * gain_e
         inner = jnp.mean(scaled * hidden, axis=-1, keepdims=True)
         grad = cot_ref[rows, :].astype(f32) + inv * scaled - hidden * (inv * inv * inv * inner)
-        ggain_ref[...] += jnp.sum(upstream * hidden * inv, axis=0, keepdims=True)
-        hg_ref[rows, :] = grad
-        low = grad.astype(bf16)
-        branch_ref[rows, :] = low
-        ag_ref[rows, :] = dot(low, wo_ref[...], NT).astype(bf16)
-        return carry
-
-    lax.fori_loop(0, tokens // step, pull, 0)
-
-    def weight(i, carry):
-        cols = pl.ds(pl.multiple_of(i * 256, 256), 256)
-        gwo_ref[:, cols] = dot(att_ref[...], branch_ref[:, cols], TN).astype(bf16)
-        return carry
-
-    lax.fori_loop(0, width // 256, weight, 0)
-
-
-def hidden_back(back, slot_col, hid, cot, att, wo, gain):
-    tokens, width = hid.shape
-    return pl.pallas_call(
-        hidden_back_kernel,
-        in_specs=[vmem()] * 7,
-        out_specs=[vmem()] * 4,
-        out_shape=[
-            jax.ShapeDtypeStruct((tokens, width), f32),
-            jax.ShapeDtypeStruct((tokens, width), bf16),
-            jax.ShapeDtypeStruct((width, width), bf16),
-            jax.ShapeDtypeStruct((1, width), f32),
-        ],
-        scratch_shapes=[pltpu.VMEM((tokens, width), bf16)],
-        compiler_params=params(),
-        name="hidden_back",
-    )(back, slot_col, hid, cot, att, wo, gain)
-
-
-def attention_backward_kernel(
-    ag_ref, att_ref, p_ref, invl_ref, q_ref, k_ref, v_ref, tok_ref, gain_ref,
-    wq_ref, wk_ref, wv_ref, gq_ref, gk_ref, gv_ref, part_ref, ggain_ref, diag_ref,
-    dq_ref, dk_ref, dv_ref, strip_ref, normed_ref, kmask_ref, vext_ref, ds_ref,
-):
-    pair = pl.program_id(0)
-    parts, seqs, span, width = tok_ref.shape
-    total = parts * span
-    table = diag_ref.shape[-1]
+        gains_ref[1:2, :] += jnp.sum(upstream * hidden * inv, axis=0, keepdims=True)
+        hid_ref[rows, :] = grad
+        grad = grad.astype(bf16)
+        cot_ref[rows, :] = grad
+        grad = dot(grad, wo_ref[...], NT).astype(bf16).reshape(seqs, span, width)
+        if k > 0:
+            agsend[src] = grad
+            ag_copy(k).start()
+        else:
+            agbuf[src] = grad
+    loads[3].wait()
+    for h in range(2):
+        cols = slice(h * 2 * rows_n, (h + 1) * 2 * rows_n)
+        grad = dot(att_ref[...].reshape(parts * block_rows, width)[:, cols], cot_ref[...], TN)
+        grad = grad.astype(bf16)
+        for t in range(2):
+            for b in range(pairs):
+                big.terms[0, 2 * h + t, b] = grad[
+                    t * rows_n : (t + 1) * rows_n, b * 128 : (b + 1) * 128
+                ]
+    big.start(0)
+    for copy in loads[4:]:
+        copy.wait()
+    for b in range(parts):
+        x = tok_ref[b].reshape(block_rows, width).astype(f32)
+        normed = x * inverse_rms(x) * gain_a
+        turned_ref[:, b * block_rows : (b + 1) * block_rows] = normed.T.astype(bf16)
+    diag_ref[...] = jnp.zeros_like(diag_ref)
+
     low, masks = half_masks(128)
     lane = lax.broadcasted_iota(jnp.int32, (1, 128), 1)
-    lanes = pl.ds(pl.multiple_of(pair * 128, 128), 128)
-    strip_ref[...] = jnp.zeros_like(strip_ref)
-
-    def one_sequence(s, carry):
-        kp = k_ref[:, s, :, lanes].reshape(total, 128)
-        vp = v_ref[:, s, :, lanes].reshape(total, 128)
-        for hh in range(2):
-            ones = (lane // 2 == 32 - 32 * hh).astype(f32)
-            kmask_ref[hh * total : (hh + 1) * total, :] = kp * masks[hh]
-            vext_ref[hh] = jnp.where(ones > 0, ones, vp.astype(f32)).astype(bf16)
-        dk = [0.0, 0.0]
-        dv = [0.0, 0.0]
-        for block in range(parts // 2):
-            rows = slice(block * 2 * span, (block + 1) * 2 * span)
-            both = slice(2 * block, 2 * block + 2)
+    strip = (parts + 2) * span
+
+    def attention_pair(phase, pair):
+        i = phase * pairs + pair
+        slot = i % 2
+        block = block_of(phase)
+        both = pl.ds(2 * block, 2)
+        lanes = pl.ds(pl.multiple_of(pair * 128, 128), 128)
+        p_copy(i).wait()
+
+        @pl.when(i + 1 < 2 * pairs)
+        def _():
+            p_copy(i + 1).start()
+
+        for s in range(seqs):
+            kp = k_ref[:, s, :, lanes].reshape(total, 128)
+            vp = v_ref[:, s, :, lanes].reshape(total, 128)
+            for hh in range(2):
+                ones = (lane // 2 == 32 - 32 * hh).astype(f32)
+                kmask_ref[hh * total : (hh + 1) * total, :] = kp * masks[hh]
+                vext_ref[hh] = jnp.where(ones > 0, ones, vp.astype(f32)).astype(bf16)
+            dk = [0.0, 0.0]
+            dv = [0.0, 0.0]
             qp = q_ref[both, s, :, lanes].reshape(2 * span, 128)
-            inv = invl_ref[both, s, :, lanes].reshape(2 * span, 128)
-            gp = ag_ref[both, s, :, lanes].reshape(2 * span, 128).astype(f32)
+            inv = invl_ref[both, s, :, lanes].reshape(2 * span, 128).astype(f32)
+            gp = agbuf[both, s, :, lanes].reshape(2 * span, 128).astype(f32)
             gp = (gp * inv).astype(bf16)
             gf = gp.astype(f32)
-            agree = gf * att_ref[both, s, :, lanes].reshape(2 * span, 128).astype(f32)
+            agree = gf * attseq_ref[both, s, :, lanes].reshape(2 * span, 128).astype(f32)
             for hh in range(2):
-                delta = -jnp.sum(
-                    jnp.where(low if hh == 0 else ~low, agree, 0.0), axis=-1, keepdims=True
-                )
+                side = low if hh == 0 else ~low
+                delta = -jnp.sum(jnp.where(side, agree, 0.0), axis=-1, keepdims=True)
                 high = delta.astype(bf16).astype(f32)
                 ext = jnp.where(lane == 64 - 64 * hh, high, 0.0)
                 ext = jnp.where(lane == 65 - 64 * hh, delta - high, ext)
-                ext = jnp.where(low if hh == 0 else ~low, gf, ext).astype(bf16)
-                raised = p_ref[0, s, rows, hh * total : (hh + 1) * total]
+                ext = jnp.where(side, gf, ext).astype(bf16)
+                raised = pbuf[slot, s, :, hh * total : (hh + 1) * total]
                 score_grad = raised.astype(f32) * dot(ext, vext_ref[hh], NT)
-                for r in range(2):
-                    at = (parts - 1 - (2 * block + r)) * span
-                    strip_ref[hh, :, at : at + total] += score_grad[r * span : (r + 1) * span]
+                if s == 0:
+                    acc_ref[hh] = score_grad
+                else:
+                    acc_ref[hh] += score_grad
                 score_grad = score_grad.astype(bf16)
                 ds_ref[:, hh * total : (hh + 1) * total] = score_grad
-                dk[hh] = dk[hh] + dot(score_grad, qp, TN)
-                dv[hh] = dv[hh] + dot(raised, gp, TN)
+                dk[hh] = dot(score_grad, qp, TN)
+                dv[hh] = dot(raised, gp, TN)
             dq = dot(ds_ref[...], kmask_ref[...])
-            at_rows = pl.ds(pl.multiple_of(s * total + block * 2 * span, 2 * span), 2 * span)
-            dq_ref[at_rows, lanes] = dq.astype(bf16)
-        rows_all = pl.ds(pl.multiple_of(s * total, total), total)
-        dk_ref[rows_all, lanes] = (jnp.where(low, dk[0], dk[1]) * (1.0 / LOG2E)).astype(bf16)
-        dv_ref[rows_all, lanes] = jnp.where(low, dv[0], dv[1]).astype(bf16)
+            q_ref[both, s, :, lanes] = dq.astype(bf16).reshape(2, span, 128)
+            dk = jnp.where(low, dk[0], dk[1]) * (1.0 / LOG2E)
+            dv = jnp.where(low, dv[0], dv[1])
+            here = slice(s * total, (s + 1) * total)
+            if phase == 0:
+                dk_ref[here, lanes] = dk
+                dv_ref[here, lanes] = dv
+            else:
+                dk = dk + dk_ref[here, lanes]
+                dv = dv + dv_ref[here, lanes]
+                k_ref[:, s, :, lanes] = dk.astype(bf16).reshape(parts, span, 128)
+                v_ref[:, s, :, lanes] = dv.astype(bf16).reshape(parts, span, 128)
+        base = pl.multiple_of((parts - 2 - 2 * block) * span, span)
+        for hh in range(2):
+            upper, lower = acc_ref[hh, :span, :], acc_ref[hh, span:, :]
+            zero = jnp.zeros((span, span), f32)
+            upper = jnp.concatenate([zero, upper, zero], axis=1)
+            lower = jnp.concatenate([lower, zero, zero], axis=1)
+            both_rows = upper + lower
+            small_sum = jnp.zeros((8, strip), f32)
+            for a in range(span // 8):
+                shift = span - 8 - 8 * a
+                rows8 = both_rows[8 * a : 8 * a + 8]
+                small_sum += rows8 if shift == 0 else pltpu.roll(rows8, shift, 1)
+            line = small_sum[7:8]
+            for a in range(7):
+                line = line + pltpu.roll(small_sum[a : a + 1], 7 - a, 1)
+            diag_ref[pl.ds(112 + 2 * pair + hh, 1), pl.ds(base, strip)] += line
+
+    ag_copy(1).wait_recv()
+
+    def first_phase(pair, carry):
+        attention_pair(0, pair)
+
+        @pl.when(pair == 1)
+        def _():
+            big.to_far(0)
+
+        @pl.when(pair == 4)
+        def _():
+            big.to_pieces(0)
+
         return carry
 
-    lax.fori_loop(0, seqs, one_sequence, 0)
-    back = lax.broadcasted_iota(jnp.int32, (span, span), 0)
-    flip = (back + lax.broadcasted_iota(jnp.int32, (span, span), 1) == span - 1).astype(f32)
-    for hh in range(2):
-        turned = lax.dot_general(
-            flip, strip_ref[hh], NN, precision=lax.Precision.HIGHEST, preferred_element_type=f32
-        )
-        turned = pltpu.roll(turned, 0, 1, stride=1, stride_axis=0)
-        diag_ref[0, hh : hh + 1, :] = jnp.sum(turned, axis=0, keepdims=True)
-
-    @pl.when(pair == pl.num_programs(0) - 1)
-    def _():
-        gain = gain_ref[...]
-        ggain_ref[...] = jnp.zeros_like(ggain_ref)
-
-        def pull(step, carry):
-            s, n = step // (parts // 2), step % (parts // 2)
-            x = tok_ref[pl.ds(2 * n, 2), s].reshape(2 * span, width).astype(f32)
-            inv = inverse_rms(x)
-            rows = pl.ds(pl.multiple_of(step * 2 * span, 2 * span), 2 * span)
-            normed_ref[rows, :] = (x * inv * gain).astype(bf16)
-            upstream = dot(dq_ref[rows, :], wq_ref[...], NT)
-            upstream += dot(dk_ref[rows, :], wk_ref[...], NT)
-            upstream += dot(dv_ref[rows, :], wv_ref[...], NT)
-            scaled = upstream * gain
-            inner = jnp.mean(scaled * x, axis=-1, keepdims=True)
-            grad = inv * scaled - x * (inv * inv * inv * inner)
-            ggain_ref[...] += jnp.sum(upstream * x * inv, axis=0, keepdims=True)
-            grad = grad.astype(bf16).reshape(2, span, width)
-            part_ref[pl.ds(2 * n, 2), s] = grad
+    lax.fori_loop(0, pairs, first_phase, 0)
+    for k in range(2, parts):
+        ag_copy(k).wait_recv()
+
+    def second_phase(j, carry):
+        def inner(t, carry):
+            attention_pair(1, 2 * j + t)
+
+            @pl.when(t == 0)
+            def _():
+                @pl.when(j > 0)
+                def _():
+                    big.to_far(j)
+
             return carry
 
-        lax.fori_loop(0, seqs * (parts // 2), pull, 0)
-
-        def weight(i, carry):
-            cols = pl.ds(pl.multiple_of(i * 256, 256), 256)
-            gq_ref[:, cols] = dot(normed_ref[...], dq_ref[:, cols], TN).astype(bf16)
-            gk_ref[:, cols] = dot(normed_ref[...], dk_ref[:, cols], TN).astype(bf16)
-            gv_ref[:, cols] = dot(normed_ref[...], dv_ref[:, cols], TN).astype(bf16)
-            return carry
-
-        lax.fori_loop(0, width // 256, weight, 0)
-
-
-def attention_backward(ag, att, p, invl, q, k, v, tok, gain, wq, wk, wv, table):
-    parts, seqs, span, width = tok.shape
-    total = parts * span
-    pairs = p.shape[0]
-    square = jax.ShapeDtypeStruct((width, width), bf16)
-    rows = pltpu.VMEM((seqs * total, width), bf16)
+        lax.fori_loop(0, 2, inner, 0)
+        cols = pl.ds(pl.multiple_of(j * 256, 256), 256)
+        for i, ref in enumerate((q_ref, k_ref, v_ref)):
+            field = ref[:, :, :, cols].reshape(parts * block_rows, 256)
+            grad = dot(turned_ref[...], field).astype(bf16)
+            for part in range(parts):
+                for t in range(2):
+                    big.terms[1 + j, part, 2 * i + t] = grad[
+                        part * rows_n : (part + 1) * rows_n, t * 128 : (t + 1) * 128
+                    ]
+        big.start(1 + j)
+
+        @pl.when(j == 0)
+        def _():
+            big.to_gather(0)
+
+        @pl.when(j > 0)
+        def _():
+            big.to_pieces(j)
+
+        return carry
+
+    lax.fori_loop(0, pairs // 2, second_phase, 0)
+
+    def part_copy(k):
+        peer = flipped(n, k, parts)
+        return remote(agsend.at[peer], partbuf.at[n], partsem, k, "narrow", peer)
+
+    for k in range(1, parts):
+        ag_copy(k).wait_send()
+    for k in range(parts - 1, -1, -1):
+        src = flipped(n, k, parts)
+        x = tok_ref[src].reshape(block_rows, width).astype(f32)
+        inv = inverse_rms(x)
+        upstream = dot(q_ref[src].reshape(block_rows, width), wq_ref[...], NT)
+        upstream += dot(k_ref[src].reshape(block_rows, width), wk_ref[...], NT)
+        upstream += dot(v_ref[src].reshape(block_rows, width), wv_ref[...], NT)
+        scaled = upstream * gain_a
+        inner = jnp.mean(scaled * x, axis=-1, keepdims=True)
+        grad = inv * scaled - x * (inv * inv * inv * inner)
+        gains_ref[0:1, :] += jnp.sum(upstream * x * inv, axis=0, keepdims=True)
+        grad = grad.astype(bf16).reshape(seqs, span, width)
+        if k > 0:
+            agsend[src] = grad
+            part_copy(k).start()
+        else:
+            partbuf[src] = grad
+        if k == 2:
+            big.to_far(3)
+        if k == 1:
+            big.to_gather(1)
+
+    pack = router_ref[...]
+    for i in range(2):
+        column = jnp.broadcast_to(gains_ref[i : i + 1, :], (128, width)).T
+        pack = pack + jnp.where(lane == 126 + i, column, 0.0)
+    relative = lax.dot_general(
+        hot_ref[...].astype(f32), diag_ref[...], NT,
+        precision=lax.Precision.HIGHEST, preferred_element_type=f32,
+    )
+    share = relative.shape[0] // parts
+    for part in range(parts):
+        slab = pack[part * rows_n : (part + 1) * rows_n]
+        head = slab[:share] + relative[part * share : (part + 1) * share]
+        small.terms[0, part, 0] = jnp.concatenate([head, slab[share:]], axis=0).astype(bf16)
+    small.start(0)
+    big.to_gather(2)
+
+    res_own.wait()
+
+    def res_wait(k, carry):
+        res_copy(k).wait()
+        return carry
+
+    lax.fori_loop(1, wide_n, res_wait, 0)
+    again = [
+        pltpu.make_async_copy(resland_any, back_ref, loadsem.at[0]),
+        pltpu.make_async_copy(hid_any, dk_ref, loadsem.at[1]),
+    ]
+    for copy in again:
+        copy.start()
+    small.to_far(0)
+    big.to_pieces(3)
+    for copy in again:
+        copy.wait()
+    outs = []
+    for b in range(parts):
+        rows = pl.ds(b * block_rows, block_rows)
+        dk_ref[rows, :] += picked(rows)
+        copy = pltpu.make_async_copy(dk_ref.at[rows], out_any.at[rows], loadsem.at[2 + b])
+        copy.start()
+        outs.append(copy)
+        if b == 0:
+            small.to_pieces(0)
+        if b == 2:
+            big.to_gather(3)
+    small.to_gather(0)
+    for k in range(parts):
+        src = flipped(n, k, parts)
+        rows = rows_of(src)
+        if k > 0:
+            part_copy(k).wait()
+        hid_ref[rows, :] += partbuf[src].reshape(block_rows, width).astype(f32)
+        copy = pltpu.make_async_copy(hid_ref.at[rows], igrad_any.at[rows], loadsem.at[6 + k])
+        copy.start()
+        outs.append(copy)
+    for g in range(4):
+        big.finish(g)
+        for b in range(pairs):
+            value = big.whole[g, b * rows_n : (b + 1) * rows_n, :].astype(f32)
+            i, at = (3, b) if g == 0 else (b // 2, 2 * (g - 1) + b % 2)
+            dv_ref[i * rows_n : (i + 1) * rows_n, at * 128 : (at + 1) * 128] = value
+    small.finish(0)
+    smallout[...] = small.whole[0, :rows_n, :].astype(f32)
+    for a, b, i in ((dv_ref.at[: 4 * rows_n], big_any, 11), (smallout, small_any, 12)):
+        copy = pltpu.make_async_copy(a, b, loadsem.at[i])
+        copy.start()
+        outs.append(copy)
+    for copy in outs:
+        copy.wait()
+
+
+def backward(args, wide_n, quad, slots_shape, table):
+    parts, seqs, span, width = quad
+    total, tokens = parts * span, parts * seqs * span
+    rows_n = width // parts
+    square = pltpu.VMEM((tokens, width), f32)
+    big_refs, big_sems = Sums.scratch(4, width // 128, rows_n, wide_n)
+    small_refs, small_sems = Sums.scratch(1, 1, rows_n, wide_n)
     return pl.pallas_call(
-        attention_backward_kernel,
-        grid=(pairs,),
-        in_specs=[
-            vmem(),
-            vmem(),
-            pl.BlockSpec((1, seqs, total, 2 * total), lambda i: (i, 0, 0, 0)),
-        ]
-        + [vmem()] * 9,
-        out_specs=[vmem()] * 5 + [pl.BlockSpec((1, 2, table), lambda i: (i, 0, 0))],
+        functools.partial(backward_kernel, wide_n),
+        in_specs=[hbm(), vmem()] + [hbm()] * 11 + [vmem()] * 8,
+        out_specs=[hbm()] * 5,
         out_shape=[
-            square, square, square,
-            jax.ShapeDtypeStruct((parts, seqs, span, width), bf16),
-            jax.ShapeDtypeStruct((1, width), f32),
-            jax.ShapeDtypeStruct((pairs, 2, table), f32),
+            jax.ShapeDtypeStruct((tokens, width), f32),
+            jax.ShapeDtypeStruct((tokens, width), f32),
+            jax.ShapeDtypeStruct((4 * rows_n, width), f32),
+            jax.ShapeDtypeStruct((rows_n, 128), f32),
+            jax.ShapeDtypeStruct(slots_shape, bf16),
         ],
         scratch_shapes=[
-            rows, rows, rows, pltpu.VMEM((2, span, table), f32), rows,
+            pltpu.VMEM(slots_shape, bf16),
+            square,
+            pltpu.VMEM((tokens, width), bf16),
+            pltpu.VMEM(quad, bf16),
+            pltpu.VMEM(quad, bf16),
+            pltpu.VMEM(quad, bf16),
+            pltpu.VMEM(quad, bf16),
+            pltpu.VMEM(quad, bf16),
+            pltpu.VMEM(quad, bf16),
+            pltpu.VMEM(quad, bf16),
+            pltpu.VMEM(quad, bf16),
+            pltpu.VMEM(quad, bf16),
+            pltpu.VMEM(quad, bf16),
+            pltpu.VMEM((width, tokens), bf16),
+            square,
+            square,
+            pltpu.VMEM((2, seqs, 2 * span, 2 * total), bf16),
+            pltpu.VMEM((2, 2 * span, total), f32),
+            pltpu.VMEM((128, table), f32),
             pltpu.VMEM((2 * total, 128), bf16),
             pltpu.VMEM((2, total, 128), bf16),
             pltpu.VMEM((2 * span, 2 * total), bf16),
-        ],
-        compiler_params=params(),
-        name="attention_backward",
-    )(ag, att, p, invl, q, k, v, tok, gain, wq, wk, wv)
-
-
-def finish_kernel(res_ref, slot_ref, hid_ref, out_ref):
-    tokens, width = hid_ref.shape
-    slots = res_ref.shape[0]
-    step = 256
-
-    def add(i, carry):
-        rows = pl.ds(pl.multiple_of(i * step, step), step)
-        ids = lax.broadcasted_iota(jnp.int32, (step, slots), 1)
-        pick = (ids == slot_ref[rows, :]).astype(f32).astype(bf16)
-        out_ref[rows, :] = hid_ref[rows, :] + dot(pick, res_ref[...])
-        return carry
-
-    lax.fori_loop(0, tokens // step, add, 0)
-
-
-def finish(res, slot_col, hid):
-    return pl.pallas_call(
-        finish_kernel,
-        in_specs=[vmem()] * 3,
-        out_specs=vmem(),
-        out_shape=jax.ShapeDtypeStruct(hid.shape, f32),
-        compiler_params=params(),
-        name="finish",
-    )(res, slot_col, hid)
+            pltpu.VMEM((8, width), f32),
+            pltpu.VMEM((rows_n, 128), f32),
+            pltpu.SemaphoreType.DMA((13,)),
+            pltpu.SemaphoreType.DMA((2,)),
+            pltpu.SemaphoreType.DMA((2, parts)),
+            pltpu.SemaphoreType.DMA((2, parts)),
+            pltpu.SemaphoreType.DMA((2, wide_n)),
+        ]
+        + big_refs
+        + small_refs
+        + big_sems
+        + small_sems,
+        compiler_params=params(collective_id=3, has_side_effects=True),
+        name="backward",
+    )(*args)
 
 
 def body(
@@ -710,15 +1006,6 @@
     gain_e = expert_gain.astype(f32).reshape(1, width)
     router = jnp.pad(router_weight, ((0, 0), (0, -experts % 128)))
 
-    def swap(array):
-        return lax.all_to_all(array, "narrow", split_axis=0, concat_axis=0, tiled=True)
-
-    def trade(array):
-        array = array.reshape(wide_n, -1, width)
-        return lax.all_to_all(array, "wide", split_axis=0, concat_axis=0, tiled=True).reshape(
-            -1, width
-        )
-
     table_ids = jnp.pad(bucket_table, (0, 1))
     offset_hot = (table_ids[None, :] == jnp.arange(buckets, dtype=jnp.int32)[:, None]).astype(bf16)
     diag = dot(relative_bias, offset_hot, TN).reshape(heads // 2, 2, table)
@@ -735,30 +1022,16 @@
         lengths, tok_quad, flat_cot, slot_row, diag * LOG2E, gain_a, gain_e,
         query_weight, key_weight, value_weight, output_weight, wide_n, cap,
     )
-    attended = att_pos.reshape(tok_count, width)
     res, back_rows, term_in, term_out, router_grad = run_experts(
         routed, slot_row, router, cot_rows, experts_in[0], experts_out[0], experts
     )
-    back_rows = back_rows.reshape(slots, width)
-    me = lax.axis_index("wide")
-    order = jnp.arange(wide_n, dtype=jnp.int32) ^ me
-    res_rows = trade(res[order])
-    hidden_grad, att_grad, output_grad, gain_second = hidden_back(
-        back_rows, slot_col, hidden, flat_cot, attended, output_weight, gain_e
-    )
-    layer_output = finish(res_rows, slot_col, hidden).reshape(seq_count, span, width)
-    ag_seq = swap(att_grad.reshape(seq_count, span, width)).reshape(narrow_n, seqs, span, width)
-    grad_query, grad_key, grad_value, part, gain_first, diag_grad = attention_backward(
-        ag_seq, att_seq, probs, invl, q, k, v, tok_seq, gain_a, query_weight, key_weight, value_weight, table
-    )
-    part = swap(part.reshape(seq_count, span, width))
-    input_grad = hidden_grad.reshape(seq_count, span, width) + part.astype(f32)
-    relative_grad = lax.dot_general(
-        offset_hot.astype(f32),
-        diag_grad.reshape(heads, table),
-        NT,
-        precision=lax.Precision.HIGHEST,
-        preferred_element_type=f32,
+    layer_output, input_grad, big, small, _ = backward(
+        (
+            back_rows, slot_col, hidden, flat_cot, att_pos, att_seq, probs, invl, q, k, v, tok_seq,
+            res, output_weight, query_weight, key_weight, value_weight, gain_a, gain_e,
+            router_grad, offset_hot,
+        ),
+        wide_n, tok_quad.shape, res.shape, table,
     )
 
     def scatter(array, dim=0):
@@ -766,29 +1039,16 @@
             array.astype(bf16), "narrow", scatter_dimension=dim, tiled=True
         ).astype(f32)
 
-    grad_experts_in = scatter(term_in)[None]
-    grad_experts_out = scatter(term_out)[None]
-    shares = tuple(
-        scatter(item)
-        for item in (
-            grad_query, grad_key, grad_value, output_grad, router_grad[:, :experts],
-            relative_grad, gain_first[0], gain_second[0],
-        )
-    )
-    totals = lax.psum(shares, "wide")
     return (
-        layer_output,
-        input_grad,
-        totals[6],
-        totals[0],
-        totals[1],
-        totals[2],
-        totals[3],
-        totals[5],
-        totals[7],
-        totals[4],
-        grad_experts_in,
-        grad_experts_out,
+        layer_output.reshape(seq_count, span, width),
+        input_grad.reshape(seq_count, span, width),
+        small[:, 126],
+        *big.reshape(narrow_n, -1, width),
+        small[: buckets // narrow_n, 112 : 112 + heads],
+        small[:, 127],
+        small[:, :experts],
+        scatter(term_in)[None],
+        scatter(term_out)[None],
     )
 
 

time: 473 us -> 353 us (0.75)
  blocking collectives: 142 us -> 0 us
  Pallas kernels: 217 us -> 307 us
  waiting for transfers between devices: 45.4 us -> 0.71 us
  starting transfers between devices: 19.4 us -> 0.08 us
  other arithmetic: 17.9 us -> 12.6 us
    psum x1 -> x0, blocking collectives: 103 us -> none  [body(): totals = lax.psum(shares, 'wide')]
    pallas_call x3 -> x1, Pallas kernels: 69.3 us -> 159 us  [backward(): pl.pallas_call(functools.partial(backward_kernel, wide_n), in_specs=[hbm(...]
    all_to_all x2 -> x0, waiting for transfers between devices: 43 us -> none  [the longest x1 22.7 us: trade(): lax.all_to_all(array, 'wide', split_axis=0, concat_axis=0, tiled=True)]
    all_to_all x1 -> x0, blocking collectives: 26.6 us -> none  [swap(): lax.all_to_all(array, 'narrow', split_axis=0, concat_axis=0, tiled=True)]
    all_to_all x2 -> x0, starting transfers between devices: 19.1 us -> none  [the longest x1 15.4 us: trade(): lax.all_to_all(array, 'wide', split_axis=0, concat_axis=0, tiled=True)]
    unnamed x1 -> x0, blocking collectives: 12 us -> none
  transfers between devices with their start and end apart: 9 -> 2, of which waited for: 2 -> 0; matrix products, arithmetic and copies ran while one was open for 3% -> 4% of each run, Pallas kernels for 15% -> 45%
where the time goes in v3:
time: 353 us
  Pallas kernels  307 us (87%)
  local copies, waits for them, and re-layouts  18.6 us (5%)
  between operations  14.1 us (4%)
  other arithmetic  12.6 us (4%)
    pallas_call x1, Pallas kernels, backward(): pl.pallas_call(functools.partial(backward_kernel, wide_n), in_specs=[hbm(...  159 us
    pallas_call x1, Pallas kernels, run_experts(): pl.pallas_call(functools.partial(expert_kernel, experts, chunks), in_spec...  92.5 us
    pallas_call x1, Pallas kernels, forward(): pl.pallas_call(functools.partial(forward_kernel, wide_n), in_specs=[pl.Bl...  55.4 us
    unnamed x12, local copies, waits for them, and re-layouts  7.14 us
  transfers between devices with their start and end apart: 2, of which 0 were waited for; matrix products, arithmetic and copies ran while one was open for 4% of the time, Pallas kernels for 45%

profile of v3, /device:TPU:0, one launch (start us, length us, event | category | flops | bytes accessed | tf_op | source)
XLA Modules:
  0.0 352.9 jit_solution(14089009538185820549)
XLA Ops:
  7.2 1.3 reshape.141.gain_a_ref
  8.5 1.3 reshape.143.gain_e_ref
  9.8 0.7 broadcast_multiply_fusion
  10.5 0.7 fusion.5
  11.1 0.7 pad.8
  11.8 2.3 reduce-window.6
  14.8 0.7 mul.38.diag_ref
  15.4 0.9 copy.30
  16.3 0.7 fusion.4
  17.6 0.7 pad.9.wr_ref
  18.3 55.4 %forward.1 = (bf16[4,2,128,768]{3,2,1,0:T(8,128)(2,1)}, bf16[4,2,128,768]{3,2,1,0:T(8,128)(2,1)}, bf16[4,2,128,768]{3,2,1,0:T(8,128)(2,1)}, f32[1024,768]{1,0:T(...) custom-call(s32[8]{0:T(128)} %lens_ref.1, ...), custom_call_target="tpu_custom_call" | custom-call | tf_op jit(solution)/shard_map/forward/pallas_call | solution.py:267
  73.7 92.5 %experts.1 = (bf16[8,160,768]{2,1,0:T(8,128)(2,1)}, bf16[8,160,768]{2,1,0:T(8,128)(2,1)}, bf16[768,3072]{1,0:T(8,128)(2,1)}, bf16[3072,768]{1,0:T(8,128)(2,1)}, f32[768,128]{1,0:T(8,128)}) custom-call(bf16[1024,768]{1,0:T(8,128)(2,1)} %get-tuple-element.32.routed_ref, s32[1,1024]{1,0:T(1,128)} %compare_select_fusion.slot_ref, bf16[768,128]{1,0:T(8,128)(2,1)} %pad.9.wr_ref, ...), custom_call_target="tpu_custom_call" | custom-call | tf_op jit(solution)/shard_map/experts/pallas_call | solution.py:445
  166.3 0.7 reduce-scatter.3.cloned.1.call-update
  168.1 0.9 add_select_fusion.slot_ref
  168.9 158.8 %backward.1 = (f32[1024,768]{1,0:T(8,128)}, f32[1024,768]{1,0:T(8,128)}, f32[768,768]{1,0:T(8,128)}, f32[192,128]{1,0:T(8,128)}, bf16[8,160,768]{2,1,0:T(8,128)(2,1)}) custom-call(bf16[8,160,768]{2,1,0:T(8,128)(2,1)} %get-tuple-element.34.back_any, s32[1024,1]{1,0:T(8,128)} %add_select_fusion.slot_ref, f32[1024,768]{1,0:T(8,128)} %get-tuple-element.35.hid_any, ...), custom_call_target="tpu_custom_call" | custom-call | tf_op jit(solution)/shard_map/backward/pallas_call | solution.py:938
  327.7 1.3 slice.25
  329.1 1.6 copy.34
  330.6 1.8 slice_reduce_fusion
  332.4 3.0 fusion.6
  335.4 2.8 bitcast_convert_fusion
  338.3 3.1 bitcast_convert_fusion.1
  341.4 1.7 copy.39
  343.0 1.4 copy-done.2
  344.4 1.7 copy.40
  (20 shorter events, 2.5 us)
Async XLA Ops:
  7.2 7.4 %copy-start = (bf16[32,12]{0,1:T(8,128)(2,1)S(1)}, bf16[32,12]{0,1:T(8,128)(2,1)}, u32[]{:S(2)}) copy-start(bf16[32,12]{0,1:T(8,128)(2,1)} %param.24) | copy-start | bytes 2308
  7.2 328.2 %reduce-scatter.5.cloned.1.call-start = ((), (), s32[]{:S(2)}) async-start(), calls=%async_computation.3 | async-start | bytes 5898240 | tf_op jit(solution)/shard_map/reduce_scatter | solution.py:1038
  166.2 172.1 %reduce-scatter.3.cloned.1.call-start = ((), (), s32[]{:S(2)}) async-start(), calls=%async_computation.2 | async-start | bytes 5898240 | tf_op jit(solution)/shard_map/reduce_scatter | solution.py:1038
  338.3 3.1 copy-start.3
  341.4 3.0 copy-start.2
  341.4 4.7 %copy-start.1 = (bf16[32,12]{0,1:T(8,128)(2,1)S(1)}, bf16[32,12]{0,1:T(8,128)(2,1)}, u32[]{:S(2)}) copy-start(bf16[32,12]{0,1:T(8,128)(2,1)} %param.24) | copy-start | bytes 2308
Sparse Core Ops, SparseCore 0:
  166.3 70.6 reduce-scatter.4
  239.7 66.5 reduce-scatter.2
